TPU v7x, 512 devices: a whole 4x4x16 slice. The times are simulated.
512 devices in a mesh: grp: 16 (over x, z_hi, core), slab: 32 (over y, z_lo).
Axes of the slice: x: 4, y: 4, z: 16 (z_hi: 2, z_lo: 8; z = z_hi * 8 + z_lo), core: 2. Of those that a mesh axis runs over, the one named last changes fastest.
Arguments:
- orbitals: bfloat16 [512, 32768], P(('grp', 'slab')), may hold values from -6 to 6
- offsets: int32 [512, 3], replicated, may hold values from 0 to 8
- slot_pairs: int32 [3072, 2], P(('grp', 'slab')), may hold values from -1 to 511, as said below
Outputs:
- exchange_field: float32 [512, 32768], P(('grp', 'slab'))
- gram: float32 [16, 32, 32], P('grp', None, 'slab')
Inputs may be any that keep to these rules, and one draw needn't show every extreme that they name: `slot_pairs`: rows 6 * d to 6 * d + 5 are the slots of device d (grp index times 32 plus slab index). A slot holds two orbital ids i != j, or -1 in both columns when empty. i lies in the slot's group (id // 32); j in the same group or in the next one (group indices wrap). Each group has exactly 160 filled slots, and some device of each group has all 6 slots filled.
All inputs are finite; a program needn't handle non-finite values.
Results may differ from a plain program's by a relative error of at most 0.0003.
Values may be sent and summed in bfloat16 or wider, within the bound.
A program may use at most 64 MiB of HBM per device.

v0:
```python
import functools
import math

import jax
import jax.numpy as jnp
from jax import lax
from jax.sharding import PartitionSpec as P

SIDE = 32
SHIFT = 8
CHEB = 6


stencil_terms = ((1, 1.5), (2, -0.15), (3, 1.0 / 90.0))
center_term = -49.0 / 18.0


def passed_along(block, axis, distance):
    devices = range(lax.axis_size(axis))
    route = [((i - distance) % len(devices), i) for i in devices]
    return lax.ppermute(block, axis, route)


def sent_together(arrays, axis, dim, along):
    ends, at = ([], 0)
    for a in arrays[:-1]:
        at += a.shape[along]
        ends.append(at)
    both = jnp.concatenate(arrays, axis=along)
    return tuple(jnp.split(lax.all_gather(both, axis, axis=dim, tiled=True), ends, axis=along))


def from_everyone(value, axis):
    size = lax.axis_size(axis)
    return lax.all_to_all(
        jnp.broadcast_to(value[None], (size, *value.shape)), axis, 0, 0, tiled=True
    )


def laid_out(blocks, dim):
    shape = list(blocks.shape[1:])
    shape[dim] *= blocks.shape[0]
    return jnp.moveaxis(blocks, 0, dim).reshape(shape)


def gather_directly(value, axis, dim):
    blocks = from_everyone(value, axis)
    return laid_out(blocks, dim)


def in_blocks(value, dim, size):
    before, after = (value.shape[:dim], value.shape[dim + 1 :])
    return jnp.moveaxis(value.reshape(*before, size, -1, *after), dim, 0)


def edges_of(length, count):
    unit = 8 if length >= 8 * count else 1
    return [length // unit * k // count * unit for k in range(1, count)]


def exchange_in_pieces(value, axis, pieces, split_dim, concat_dim):
    blocks = in_blocks(value, split_dim, lax.axis_size(axis))
    cut = max(range(1, max(2, blocks.ndim - 1)), key=lambda d: blocks.shape[d])
    finished = []
    for piece in jnp.split(blocks, edges_of(blocks.shape[cut], pieces), axis=cut):
        if piece.size:
            finished.append(lax.all_to_all(piece, axis, split_axis=0, concat_axis=0, tiled=True))
    return laid_out(jnp.concatenate(finished, axis=cut), concat_dim)


def summed_on_arrival(value, axis, dim):
    size = lax.axis_size(axis)
    blocks = lax.all_to_all(in_blocks(value, dim, size), axis, 0, 0, tiled=True)
    return jnp.sum(blocks, axis=0)


def slide_cells(values, offset, dim_index):
    extent = values.shape[dim_index]
    pad_shape = list(values.shape)
    pad_shape[dim_index] = abs(offset)
    zero_part = jnp.zeros(pad_shape, values.dtype)
    if offset > 0:
        kept_part = lax.slice_in_dim(values, offset, extent, axis=dim_index)
        return jnp.concatenate((kept_part, zero_part), dim_index)
    kept_part = lax.slice_in_dim(values, 0, extent + offset, axis=dim_index)
    return jnp.concatenate((zero_part, kept_part), dim_index)


def operator(values, box_edge):
    outer_dim = values.ndim - 2
    inner_dim = values.ndim - 1
    zcoord = lax.broadcasted_iota(jnp.int32, (box_edge * box_edge,), 0) % box_edge
    stencil_sum = 3.0 * center_term * values
    for offset, weight in stencil_terms:
        beside = slide_cells(values, offset, outer_dim) + slide_cells(values, -offset, outer_dim)
        beside = (
            beside
            + slide_cells(values, offset * box_edge, inner_dim)
            + slide_cells(values, -offset * box_edge, inner_dim)
        )
        upper_part = jnp.where(
            zcoord + offset < box_edge, slide_cells(values, offset, inner_dim), 0.0
        )
        lower_part = jnp.where(zcoord - offset >= 0, slide_cells(values, -offset, inner_dim), 0.0)
        stencil_sum = stencil_sum + weight * (beside + upper_part + lower_part)
    return -stencil_sum


def coefficients(box_edge, sweeps):
    lowest = 3.0 * (math.pi / (box_edge + 1)) ** 2
    highest = 18.2
    center_value = 0.5 * (highest + lowest)
    half_width = 0.5 * (highest - lowest)
    alpha_list = [1.0 / center_value]
    beta_list = [0.0]
    for step_index in range(1, sweeps):
        previous = alpha_list[-1]
        if step_index == 1:
            beta_now = 0.5 * (half_width * previous) ** 2
        else:
            beta_now = (0.5 * half_width * previous) ** 2
        alpha_list.append(1.0 / (center_value - beta_now / previous))
        beta_list.append(beta_now)
    return (alpha_list, beta_list)


def chebyshev_solve(density, box_edge, sweeps):
    alpha_list, beta_list = coefficients(box_edge, sweeps)
    alpha_table = jnp.asarray(alpha_list, jnp.float32)
    beta_table = jnp.asarray(beta_list, jnp.float32)

    def advance(step_index, state):
        solution, residual, search = state
        search = residual + beta_table[step_index] * search
        solution = solution + alpha_table[step_index] * search
        residual = residual - alpha_table[step_index] * operator(search, box_edge)
        return (solution, residual, search)

    start = (jnp.zeros_like(density), density, jnp.zeros_like(density))
    return lax.fori_loop(0, sweeps, advance, start)[0]


def place_box(box, offset_gap, box_edge, margin):
    cube = box.reshape(box_edge, box_edge, box_edge)
    padded = jnp.pad(cube, margin)
    start = margin - offset_gap
    moved = lax.dynamic_slice(
        padded, (start[0], start[1], start[2]), (box_edge, box_edge, box_edge)
    )
    return moved.reshape(box_edge, box_edge * box_edge)


def on_device(orbitals, offsets, slot_pairs):
    box_edge = SIDE
    cell_count = orbitals.shape[1]
    shaped = functools.partial(place_box, box_edge=box_edge, margin=SHIFT)
    members = lax.axis_size("slab")
    group_count = lax.axis_size("grp")
    group_index = lax.axis_index("grp")
    member_index = lax.axis_index("slab")
    next_box = passed_along(orbitals, "grp", -1)
    near_boxes, far_boxes = sent_together((orbitals, next_box), "slab", 0, 1)
    listing = gather_directly(slot_pairs, "slab", 0)
    live_flags = listing[:, 0] >= 0
    live_ranks = jnp.cumsum(live_flags.astype(jnp.int32)) - 1
    slot_quota = -(-(5 * members) // members)
    targets = member_index * slot_quota + jnp.arange(slot_quota, dtype=jnp.int32)
    select = live_flags[None, :] & (live_ranks[None, :] == targets[:, None])
    chosen_pairs = jnp.sum(jnp.where(select[:, :, None], listing[None, :, :], 0), axis=1)
    live_slot = jnp.any(select, axis=1)
    first_id = group_index * members
    second_id = (group_index + 1) % group_count * members
    own_id = first_id + member_index
    left_id = jnp.where(live_slot, chosen_pairs[:, 0], own_id)
    right_id = jnp.where(live_slot, chosen_pairs[:, 1], own_id)
    left_row = left_id - first_id
    right_row = jnp.where(
        right_id // members == group_index, right_id - first_id, members + right_id - second_id
    )
    box_table = jnp.concatenate((near_boxes, far_boxes), 0)
    offset_gap = offsets[right_id] - offsets[left_id]
    left_box = box_table[left_row].reshape(-1, box_edge, box_edge * box_edge).astype(jnp.float32)
    right_box = jax.vmap(shaped)(box_table[right_row], offset_gap).astype(jnp.float32)
    density = left_box * right_box * live_slot.astype(jnp.float32)[:, None, None]
    potential = chebyshev_solve(density, box_edge, CHEB)
    to_left = (potential * right_box).reshape(-1, cell_count)
    to_right = jax.vmap(shaped)(potential * left_box, -offset_gap).reshape(-1, cell_count)
    partial_fields = jnp.zeros((2 * members, cell_count), jnp.float32)
    partial_fields = partial_fields.at[left_row].add(to_left).at[right_row].add(to_right)
    incoming = passed_along(partial_fields[members:], "grp", 1)
    merged = exchange_in_pieces(partial_fields[:members] + incoming, "slab", 2, 0, 0)
    exchange_field = jnp.sum(merged, 0, keepdims=True)
    anchor = offsets[first_id]
    own_shift = offsets[own_id] - anchor
    framed_field = shaped(exchange_field[0], own_shift).astype(jnp.bfloat16).reshape(1, cell_count)
    norm_factor = 1.0 / math.sqrt(cell_count)
    framed_orbital = shaped(orbitals[0], own_shift).reshape(1, cell_count)
    orbital_slabs, field_slabs = (
        lax.all_to_all(framed_orbital, "slab", split_axis=1, concat_axis=0, tiled=True),
        lax.all_to_all(framed_field, "slab", split_axis=1, concat_axis=0, tiled=True),
    )
    partial_gram = (
        lax.dot_general(
            orbital_slabs, field_slabs, (((1,), (1,)), ((), ())), preferred_element_type=jnp.float32
        )
        * norm_factor
    )
    column = summed_on_arrival(partial_gram, "slab", 1)
    gram_block = column.reshape(1, members, 1)
    return (exchange_field, gram_block)


def solution(mesh):
    return jax.shard_map(
        on_device,
        mesh=mesh,
        in_specs=(P(("grp", "slab"), None), P(), P(("grp", "slab"), None)),
        out_specs=(P(("grp", "slab"), None), P("grp", None, "slab")),
        check_vma=False,
    )
```

profile of v0, /device:TPU:6, one launch (start us, length us, event | category | flops | bytes accessed | tf_op | source)
XLA Modules:
  0.0 872.9 jit_solution(8631526173494886654)
XLA Ops:
  7.2 15.4 %collective-permute-start = (bf16[1,32768]{1,0:T(2,128)(2,1)}, bf16[1,32768]{1,0:T(2,128)(2,1)S(1)}, u32[]{:S(2)}, u32[]{:S(2)}) collective-permute-start(bf16[1,32768]{1,0:T(2,128)(2,1)} %param.7), channel_id=1, source_target_pairs={{32,0},{64,32},{96,64},{128,96},{160,128},{192,160},{224,192},{256... | collective-permute-start | bytes 196616 | tf_op jit(solution)/shard_map/ppermute | solution.py:21
  28.9 9.2 %all-to-all-start = ((s32[32,6,2]{1,2,0:T(2,128)}), s32[32,6,2]{1,2,0:T(2,128)S(1)}, u32[]{:S(2)}, u32[]{:S(2)}) async-start(s32[32,6,2]{1,2,0:T(2,128)} %broadcast_in_dim.132), calls=%async_computation | async-start | bytes 65536 | tf_op jit(solution)/shard_map/all_to_all | solution.py:35
  39.1 11.6 %all-to-all-done = s32[32,6,2]{1,2,0:T(2,128)S(1)} async-done(((s32[32,6,2]{1,2,0:T(2,128)}), s32[32,6,2]{1,2,0:T(2,128)S(1)}, u32[]{:S(2)}, u32[]{:S(2)}) %all-to-all-start) | async-done | bytes 1568 | tf_op jit(solution)/shard_map/all_to_all | solution.py:35
  53.6 238.1 %all-gather.3.cloned.1.call-done = bf16[32,1,65536]{2,1,0:T(2,128)(2,1)} async-done(((bf16[1,1,65536]{2,1,0:T(2,128)(2,1)}), bf16[32,1,65536]{2,1,0:T(2,128)(2,1)}) %all-gather.3.cloned.1.call-update) | async-done | bytes 4194320 | tf_op jit(solution)/shard_map/all_gather | solution.py:30
  291.7 8.0 copy.77
  302.1 3.8 gather_fusion.1
  309.1 25.1 %while.23 = (s32[]{:T(128)}, bf16[5,48,48,48]{3,2,1,0:T(8,128)(2,1)}, s32[5,4]{1,0:T(8,128)S(1)}, bf16[5,32,32,32]{3,2,1,0:T(8,128)(2,1)}, s32[]{:T(128)}) while((s32[]{:T(128)}, bf16[5,48,48,48]{3,2,1,0:T(8,128)(2,1)}, s32[5,4]{1,0:T(8,128)S(1)}, bf16[5,32,32,32]{3,2,1,0:T(8,128)(2,1)}, s32[]{:T(128)}) %tuple.145), condition=%wide.while_cond, body=%wide.while_body.sunk | while | flops 2 | bytes 526977 | solution.py:147
  309.8 4.4 dynamic-slice_dynamic-update-slice_fusion.4
  314.8 4.4 dynamic-slice_dynamic-update-slice_fusion.4
  319.8 4.4 dynamic-slice_dynamic-update-slice_fusion.4
  324.8 4.3 dynamic-slice_dynamic-update-slice_fusion.4
  329.8 4.4 dynamic-slice_dynamic-update-slice_fusion.4
  337.5 3.8 gather_fusion
  342.9 42.8 %while.25 = (s32[]{:T(128)}, f32[5,32,1024]{2,1,0:T(8,128)S(1)}, f32[5,32,1024]{2,1,0:T(8,128)S(1)}, f32[5,32,1024]{2,1,0:T(8,128)S(1)}, s32[]{:T(128)}, /*index=5*/f32[6]{0:T(128)S(1)}, s32[]{:T(128)}, f32[6]{0:T(128)S(1)}) while((s32[]{:T(128)}, f32[5,32,1024]{2,1,0:T(8,128)S(1)}, f32[5,32,1024]{2,1,0:T(8,128)S(1)}, ...), condition=%wide.region_5.6_spmd.clone.clone, body=%wide.region_4.5_spmd.sunk.clone.clone.sunk | while | flops 6092803 | bytes 39147136 | solution.py:140
  393.9 26.0 %while.24 = (s32[]{:T(128)}, f32[5,48,48,48]{3,2,1,0:T(8,128)}, s32[5,4]{1,0:T(8,128)S(1)}, f32[5,32,32,32]{3,2,1,0:T(8,128)}, s32[]{:T(128)}) while((s32[]{:T(128)}, f32[5,48,48,48]{3,2,1,0:T(8,128)}, s32[5,4]{1,0:T(8,128)S(1)}, f32[5,32,32,32]{3,2,1,0:T(8,128)}, s32[]{:T(128)}) %tuple.151), condition=%wide.while_cond.1, body=%wide.while_body.1.sunk | while | flops 2 | bytes 1051265 | solution.py:147
  394.5 4.6 dynamic-slice_dynamic-update-slice_fusion.5
  399.7 4.6 dynamic-slice_dynamic-update-slice_fusion.5
  404.9 4.6 dynamic-slice_dynamic-update-slice_fusion.5
  410.1 4.6 dynamic-slice_dynamic-update-slice_fusion.5
  415.2 4.6 dynamic-slice_dynamic-update-slice_fusion.5
  423.1 5.0 scatter_custom_fusion
  428.1 8.1 scatter_fusion
  440.9 104.7 %collective-permute-done.1 = f32[32,32768]{1,0:T(8,128)S(1)} collective-permute-done((f32[32,32768]{1,0:T(8,128)S(1)}, f32[32,32768]{1,0:T(8,128)S(1)}, u32[]{:S(2)}, u32[]{:S(2)}) %collective-permute-start.1) | collective-permute-done | bytes 4194336 | tf_op jit(solution)/shard_map/ppermute | solution.py:21
  546.1 4.0 reshape.153
  550.1 81.1 %all-to-all-start.1 = ((f32[32,1,32768]{2,1,0:T(1,128)}), f32[32,1,32768]{2,1,0:T(1,128)}, u32[]{:S(2)}, u32[]{:S(2)}) async-start(f32[32,1,32768]{2,1,0:T(1,128)} %reshape.153), calls=%async_computation.1 | async-start | bytes 8388608 | tf_op jit(solution)/shard_map/all_to_all | solution.py:67
  640.8 161.2 %all-to-all-done.1 = f32[32,1,32768]{2,1,0:T(1,128)} async-done(((f32[32,1,32768]{2,1,0:T(1,128)}), f32[32,1,32768]{2,1,0:T(1,128)}, u32[]{:S(2)}, u32[]{:S(2)}) %all-to-all-start.1) | async-done | bytes 4194336 | tf_op jit(solution)/shard_map/all_to_all | solution.py:67
  802.1 14.3 %all-to-all-start.2 = ((bf16[32,2,512]{2,1,0:T(2,128)(2,1)}), bf16[32,2,512]{2,1,0:T(2,128)(2,1)S(1)}, u32[]{:S(2)}, u32[]{:S(2)}) async-start(bf16[32,2,512]{2,1,0:T(2,128)(2,1)} %reshape.274), calls=%async_computation.2 | async-start | bytes 131072 | tf_op jit(solution)/shard_map/all_to_all | solution.py:199
  816.4 4.9 reduce_sum.28
  823.8 5.2 all-to-all-done.2
  829.0 7.3 all-to-all-start.3
  836.4 12.6 %all-to-all-done.3 = bf16[32,2,512]{2,1,0:T(2,128)(2,1)S(1)} async-done(((bf16[32,2,512]{2,1,0:T(2,128)(2,1)}), bf16[32,2,512]{2,1,0:T(2,128)(2,1)S(1)}, u32[]{:S(2)}, u32[]{:S(2)}) %all-to-all-start.3) | async-done | bytes 65568 | tf_op jit(solution)/shard_map/all_to_all | solution.py:200
  849.3 16.2 %all_to_all.45 = f32[32,32,1]{1,2,0:T(1,128)S(1)} all-to-all(f32[32,32,1]{1,2,0:T(1,128)S(1)} %copy.50), channel_id=1, replica_groups=mesh['grp'=16,'slab'=32] {'slab'}, dimensions={0} | all-to-all | bytes 8192 | tf_op jit(solution)/shard_map/all_to_all | solution.py:73
  (199 shorter events, 93.1 us)
Async XLA Ops:
  7.2 284.5 %all-gather.3.cloned.1.call-start = ((), (), s32[]{:S(2)}) async-start(), calls=%async_computation.5 | async-start | bytes 8650752 | tf_op jit(solution)/shard_map/all_gather | solution.py:30
  7.2 18.5 %collective-permute-start = (bf16[1,32768]{1,0:T(2,128)(2,1)}, bf16[1,32768]{1,0:T(2,128)(2,1)S(1)}, u32[]{:S(2)}, u32[]{:S(2)}) collective-permute-start(bf16[1,32768]{1,0:T(2,128)(2,1)} %param.7), channel_id=1, source_target_pairs={{32,0},{64,32},{96,64},{128,96},{160,128},{192,160},{224,192},{256... | collective-permute-start | bytes 196616 | tf_op jit(solution)/shard_map/ppermute | solution.py:21
  28.9 21.8 %all-to-all-start = ((s32[32,6,2]{1,2,0:T(2,128)}), s32[32,6,2]{1,2,0:T(2,128)S(1)}, u32[]{:S(2)}, u32[]{:S(2)}) async-start(s32[32,6,2]{1,2,0:T(2,128)} %broadcast_in_dim.132), calls=%async_computation | async-start | bytes 65536 | tf_op jit(solution)/shard_map/all_to_all | solution.py:35
  337.5 5.4 copy-start.5
  337.5 5.4 copy-start.6
  393.9 28.8 %copy-start.1 = (f32[1,5,32,1024]{3,2,1,0:T(8,128)S(1)}, f32[1,5,32,1024]{3,2,1,0:T(8,128)}, u32[]{:S(2)}) copy-start(f32[1,5,32,1024]{3,2,1,0:T(8,128)} %get-tuple-element.316) | copy-start | bytes 1966084
  436.1 109.5 %copy-start = (f32[64,32768]{1,0:T(8,128)S(1)}, f32[64,32768]{1,0:T(8,128)}, u32[]{:S(2)}) copy-start(f32[64,32768]{1,0:T(8,128)} %scatter_fusion) | copy-start | bytes 25165828
  438.8 106.9 %collective-permute-start.1 = (f32[32,32768]{1,0:T(8,128)S(1)}, f32[32,32768]{1,0:T(8,128)S(1)}, u32[]{:S(2)}, u32[]{:S(2)}) collective-permute-start(f32[32,32768]{1,0:T(8,128)S(1)} %slice.373), channel_id=1, source_target_pairs={{480,0},{0,32},{32,64},{64,96},{96,128},{128,160},{160,192},{192,2... | collective-permute-start | bytes 12582920 | tf_op jit(solution)/shard_map/ppermute | solution.py:21
  550.1 81.1 %copy-start.4 = (s32[512,3]{0,1:T(4,128)S(1)}, s32[512,3]{0,1:T(4,128)}, u32[]{:S(2)}) copy-start(s32[512,3]{0,1:T(4,128)} %param.8) | copy-start | bytes 18436
  550.1 85.4 %copy-start.3 = (bf16[1,32768]{1,0:T(2,128)(2,1)S(1)}, bf16[1,32768]{1,0:T(2,128)(2,1)}, u32[]{:S(2)}) copy-start(bf16[1,32768]{1,0:T(2,128)(2,1)} %param.7) | copy-start | bytes 196612
  550.1 251.9 %all-to-all-start.1 = ((f32[32,1,32768]{2,1,0:T(1,128)}), f32[32,1,32768]{2,1,0:T(1,128)}, u32[]{:S(2)}, u32[]{:S(2)}) async-start(f32[32,1,32768]{2,1,0:T(1,128)} %reshape.153), calls=%async_computation.1 | async-start | bytes 8388608 | tf_op jit(solution)/shard_map/all_to_all | solution.py:67
  802.1 27.0 %all-to-all-start.2 = ((bf16[32,2,512]{2,1,0:T(2,128)(2,1)}), bf16[32,2,512]{2,1,0:T(2,128)(2,1)S(1)}, u32[]{:S(2)}, u32[]{:S(2)}) async-start(bf16[32,2,512]{2,1,0:T(2,128)(2,1)} %reshape.274), calls=%async_computation.2 | async-start | bytes 131072 | tf_op jit(solution)/shard_map/all_to_all | solution.py:199
  821.3 44.7 %copy-start.2 = (f32[32768]{0:T(1024)}, f32[32768]{0:T(1024)S(1)}, u32[]{:S(2)}) copy-start(f32[32768]{0:T(1024)S(1)} %reduce_sum.28) | copy-start | bytes 393220
  829.0 20.0 %all-to-all-start.3 = ((bf16[32,2,512]{2,1,0:T(2,128)(2,1)}), bf16[32,2,512]{2,1,0:T(2,128)(2,1)S(1)}, u32[]{:S(2)}, u32[]{:S(2)}) async-start(bf16[32,2,512]{2,1,0:T(2,128)(2,1)} %reshape.272), calls=%async_computation.3 | async-start | bytes 131072 | tf_op jit(solution)/shard_map/all_to_all | solution.py:200
Sparse Core Ops, SparseCore 0:
  27.7 263.8 all-gather.2
where the time goes:
time: 875 us; the launch traced here: 873 us
  waiting for transfers between devices  537 us (61%)
  starting transfers between devices  130 us (15%)
  local copies, waits for them, and re-layouts  114 us (13%)
  other arithmetic  55.6 us (6%)
  between operations  20 us (2%)
  blocking collectives  16.2 us (2%)
    all_gather x1, waiting for transfers between devices, sent_together(): lax.all_gather(both, axis, axis=dim, tiled=True)  238 us
    all_to_all x1, waiting for transfers between devices, exchange_in_pieces(): lax.all_to_all(piece, axis, split_axis=0, concat_axis=0, tiled=True)  161 us
    ppermute x2, waiting for transfers between devices, passed_along(): return lax.ppermute(block, axis, route)  108 us
    all_to_all x1, starting transfers between devices, exchange_in_pieces(): lax.all_to_all(piece, axis, split_axis=0, concat_axis=0, tiled=True)  81.1 us
    gather x30, local copies, waits for them, and re-layouts  51 us
    ppermute x2, starting transfers between devices, passed_along(): return lax.ppermute(block, axis, route)  17.6 us
  transfers between devices with their start and end apart: 7, of which 7 were waited for; matrix products, arithmetic and copies ran while one was open for 2% of the time, Pallas kernels for 0%

commit v1 on v0

v1 whole, which is shorter than its diff:
```python
import math

import jax
import jax.numpy as jnp
import numpy as np
from jax import lax
from jax.experimental import pallas as pl
from jax.experimental.pallas import tpu as pltpu
from jax.sharding import PartitionSpec as P

SIDE = 32
PLANE = SIDE * SIDE
CELLS = SIDE * PLANE
CHEB = 6
GROUPS = 16
ORB = 32
PAIRS = 160
PART = 40
BLOCK = 32
F32, BF16, I32 = jnp.float32, jnp.bfloat16, jnp.int32
MESH = pl.DeviceIdType.MESH

NN = (((1,), (0,)), ((), ()))
NT = (((1,), (1,)), ((), ()))
TN = (((0,), (0,)), ((), ()))


def operator_1d():
    weights = {0: -49.0 / 18.0, 1: 1.5, 2: -0.15, 3: 1.0 / 90.0}
    a = np.zeros((SIDE, SIDE))
    for i in range(SIDE):
        for j in range(SIDE):
            a[i, j] = -weights.get(abs(i - j), 0.0)
    return a


def eigen(a):
    a, n = a.copy(), a.shape[0]
    v = np.eye(n)
    for _ in range(10):
        for p in range(n - 1):
            for q in range(p + 1, n):
                if abs(a[p, q]) < 1e-18:
                    continue
                theta = (a[q, q] - a[p, p]) / (2.0 * a[p, q])
                t = (1.0 if theta >= 0 else -1.0) / (abs(theta) + math.sqrt(theta * theta + 1.0))
                c = 1.0 / math.sqrt(t * t + 1.0)
                s = t * c
                ap, aq = a[:, p].copy(), a[:, q].copy()
                a[:, p], a[:, q] = c * ap - s * aq, s * ap + c * aq
                ap, aq = a[p].copy(), a[q].copy()
                a[p], a[q] = c * ap - s * aq, s * ap + c * aq
                vp, vq = v[:, p].copy(), v[:, q].copy()
                v[:, p], v[:, q] = c * vp - s * vq, s * vp + c * vq
    return np.diag(a).copy(), v


def polynomial(lam):
    low, high = 3.0 * (math.pi / (SIDE + 1)) ** 2, 18.2
    mid, half = 0.5 * (high + low), 0.5 * (high - low)
    alpha, beta = 1.0 / mid, 0.0
    x, res, p = np.zeros_like(lam), np.ones_like(lam), np.zeros_like(lam)
    for k in range(1, CHEB + 1):
        if k > 1:
            beta = 0.5 * (half * alpha) ** 2 if k == 2 else (0.5 * half * alpha) ** 2
            alpha = 1.0 / (mid - beta / alpha)
        p = res + beta * p
        x = x + alpha * p
        res = res - alpha * lam * p
    return x


def halves(a):
    high = a.astype(BF16)
    low = (a - high.astype(np.float64)).astype(BF16)
    return np.stack([high, low])


def constants():
    lam, q = eigen(operator_1d())
    plane = halves(np.kron(q, q))
    lines = halves(np.stack([np.kron(q.T, np.eye(8)), np.kron(q, np.eye(8))]))
    total = lam[:, None, None] + lam[None, :, None] + lam[None, None, :]
    table = polynomial(total).reshape(SIDE, PLANE).astype(np.float32)
    return plane, lines, table


def iota(shape, dim):
    return lax.broadcasted_iota(I32, shape, dim)


def roll(x, n, axis):
    n %= x.shape[axis]
    return pltpu.roll(x, n, axis) if n else x


def lead(x, n):
    n %= x.shape[0]
    return jnp.concatenate([x[x.shape[0] - n :], x[: x.shape[0] - n]], 0) if n else x


def bit(o, b):
    return jnp.bitwise_and(jnp.right_shift(o, b), 1) > 0


def turn_rows(x, o2, o3, sign):
    third = jnp.bitwise_and(iota(x.shape, 1), SIDE - 1)
    b2 = jnp.broadcast_to(o2, x.shape)
    b3 = jnp.broadcast_to(o3, x.shape)
    for b in range(4):
        n = 1 << b
        x = jnp.where(bit(b2, b), roll(x, sign * SIDE * n, 1), x)
        inside = third >= n if sign > 0 else third < SIDE - n
        y = jnp.where(inside, roll(x, sign * n, 1), roll(x, sign * (n - SIDE), 1))
        x = jnp.where(bit(b3, b), y, x)
    return x


def turn_box(x, o, sign):
    o1, o2, o3 = (jnp.broadcast_to(v, x.shape) for v in o)
    lane = iota(x.shape, 2)
    third = jnp.bitwise_and(lane, SIDE - 1)
    for b in range(4):
        n = 1 << b
        x = jnp.where(bit(o1, b), lead(x, sign * n), x)
        if b < 2:
            y = roll(x, sign * SIDE * n, 2)
            kept = lane >= SIDE * n if sign > 0 else lane < 128 - SIDE * n
            y = jnp.where(kept, y, roll(y, sign, 1))
        else:
            y = roll(x, sign * n // 4, 1)
        x = jnp.where(bit(o2, b), y, x)
        inside = third >= n if sign > 0 else third < SIDE - n
        y = jnp.where(inside, roll(x, sign * n, 2), roll(x, sign * (n - SIDE), 2))
        x = jnp.where(bit(o3, b), y, x)
    return x


def turn_lead(x, o1, sign):
    o = jnp.broadcast_to(o1, x.shape[1:])[None]
    for b in range(4):
        x = jnp.where(bit(o, b), lead(x, sign << b if sign > 0 else -(1 << b)), x)
    return x


def split(x):
    high = x.astype(BF16)
    return high, (x - high.astype(F32)).astype(BF16)


def dot(a, b, dims=NN):
    return lax.dot_general(a, b, dims, preferred_element_type=F32)


def device(x, y, z, c):
    return x * 4 + lax.div(z, 8) * 2 + c, y * 8 + lax.rem(z, 8)


def kernel(
    box_ref, offsets_ref, slots_ref, plane_ref, lines_ref, table_ref,
    field_ref, gram_ref,
    plane, lines, own, mid, near_out, far_out, near_in, far_in, cells,
    ohl, ohr, offs, lm, rm, dh, dl, modes, lines_in, lines_out, back,
    field, far_field, prev_field, tiles, gp, send6, mid6, send7, fin,
    const_sem, send1, recv1, send2, recv2, send3, recv3, send4, recv4, send5, recv5, send6s, recv6, send7s, recv7,
):
    gi, si = lax.axis_index("grp"), lax.axis_index("slab")
    x, zh, core = lax.div(gi, 4), lax.rem(lax.div(gi, 2), 2), lax.rem(gi, 2)
    y, zl = lax.div(si, 8), lax.rem(si, 8)
    z = zh * 8 + zl
    q = x * 4 + y
    rho = q * 2 + core
    role = z
    nxt = lax.rem(role + 1, GROUPS)

    const1 = pltpu.make_async_copy(plane_ref, plane, const_sem.at[0])
    const2 = pltpu.make_async_copy(lines_ref, lines, const_sem.at[1])
    const1.start()
    const2.start()

    row = iota((72, 512), 0)
    local = lax.rem(row, ORB)
    ident = jnp.where(row < ORB, role, nxt) * ORB + lax.rem(local, 4) * 8 + lax.div(local, 4)
    ident = jnp.where(row < 2 * ORB, ident, gi * ORB + si)
    pick = (ident == iota((72, 512), 1)).astype(BF16)
    found = dot(pick, offsets_ref[...].astype(BF16))
    own_o = [found[64:65, d : d + 1].astype(I32).reshape(1, 1, 1) for d in range(3)]

    box = turn_box(box_ref[...].astype(F32).reshape(SIDE, 8, 128), own_o, 1)
    own[:, 0] = box.reshape(16, 16, 128).astype(BF16)
    slots = slots_ref[...]
    member = lax.rem(slots, ORB)
    spot = lax.rem(member, 8) * 4 + lax.div(member, 8)
    spot = spot + jnp.where(lax.div(slots, ORB) == gi, 0, ORB)
    spot = jnp.where(slots >= 0, spot, -1).astype(F32)
    own[:, 1] = jnp.broadcast_to(jnp.concatenate([spot, spot], 0).astype(BF16)[None], (16, 16, 128))

    pltpu.make_async_copy(own.at[q], mid.at[q], recv1).start()
    for t in range(1, 16):
        peer = lax.rem(q + t, 16)
        pltpu.make_async_remote_copy(
            own.at[peer], mid.at[q], send1, recv1, device(lax.div(peer, 4), lax.rem(peer, 4), z, core), MESH
        ).start()
    pltpu.make_async_copy(mid, mid, recv1).wait()

    heap = mid[:, 0].astype(F32).reshape(4, 4, 2, 8, 128)
    lists = mid[:, 1].astype(F32)[:, :8].reshape(4, 4, 8, 128)
    lane8 = iota((8, 128), 1)
    for g in range(4):
        merged = lists[g, 0]
        for j in range(1, 4):
            merged = jnp.where(lax.div(lane8, 2) == j, roll(lists[g, j], 2 * j, 1), merged)
        merged = jnp.concatenate([merged, merged], 0).astype(BF16)
        for c in range(2):
            part = heap[g, :, c].reshape(2, 16, 128).astype(BF16)
            near_out[g, c, 0:2] = part
            near_out[g, c, 2] = merged
            far_out[g, c] = part
    sends2 = []
    for g in range(4):
        for c in range(2):
            for far in range(2):
                target = lax.rem(g * 4 + zh * 2 + core + GROUPS - far, GROUPS)
                here = jnp.logical_and(target == z, core == c)
                out = (near_out, far_out)[far].at[g, c]
                into = (near_in, far_in)[far].at[zl]
                remote = pltpu.make_async_remote_copy(
                    out, into, send2.at[g, c, far], recv2.at[far], device(x, y, target, c), MESH
                )
                local_copy = pltpu.make_async_copy(out, into, recv2.at[far])
                pl.when(here)(local_copy.start)
                pl.when(jnp.logical_not(here))(remote.start)
                sends2.append((here, remote))
    pltpu.make_async_copy(own.at[pl.ds(0, 15)], own.at[pl.ds(0, 15)], send1).wait()
    pltpu.make_async_copy(near_in, near_in, recv2.at[0]).wait()
    pltpu.make_async_copy(far_in, far_in, recv2.at[1]).wait()

    lists = near_in[:, 2].astype(F32)[:, :8].reshape(64, 128)
    left = jnp.concatenate([lists[:, 2 * j : 2 * j + 1] for j in range(4)], 0)
    right = jnp.concatenate([lists[:, 2 * j + 1 : 2 * j + 2] for j in range(4)], 0)
    row = iota((64, 1), 0)
    used = lax.rem(row, 8) < 6
    used = jnp.concatenate([used.astype(F32)] * 4, 0)
    live = jnp.logical_and(left >= 0, used > 0)
    live_f = jnp.where(live, 1.0, 0.0)
    before = (iota((256, 256), 1) < iota((256, 256), 0)).astype(BF16)
    rank = dot(before, jnp.broadcast_to(live_f, (256, 128)).astype(BF16))[:, 0:1]
    rank = jnp.where(live, rank, -1.0)
    chosen = (jnp.broadcast_to(rank, (256, 256)) == iota((256, 256), 1).astype(F32)).astype(BF16)
    orbital = iota((256, 128), 1).astype(F32)
    pick_l = (jnp.broadcast_to(left, (256, 128)) == orbital).astype(BF16)
    pick_r = (jnp.broadcast_to(right, (256, 128)) == orbital).astype(BF16)
    one_l = dot(chosen, pick_l, TN)[:PAIRS]
    one_r = dot(chosen, pick_r, TN)[:PAIRS]
    ohl[...] = one_l
    ohr[...] = one_r
    o3 = jnp.concatenate([found[:64], jnp.zeros((64, found.shape[1]), F32)], 0)
    offs[...] = jnp.broadcast_to(dot(one_l.astype(BF16), o3.astype(BF16))[:, :3], (PAIRS, 3)).astype(I32)

    cells[0:256] = near_in[:, 0:2].astype(F32).reshape(256, 128)
    cells[256:512] = far_in[...].astype(F32).reshape(256, 128)
    orbs = jnp.concatenate([cells[pl.ds(r, 64, stride=8), :] for r in range(8)], 1)
    lane = iota((64, PLANE), 1)
    o = [jnp.broadcast_to(found[:64, d : d + 1], (64, PLANE)) for d in range(3)]
    code = jnp.where(rho.astype(F32) < o[0], 1.0, 0.0)
    code = code + jnp.where(lax.div(lane, SIDE).astype(F32) < o[1], 2.0, 0.0)
    code = code + jnp.where(jnp.bitwise_and(lane, SIDE - 1).astype(F32) < o[2], 4.0, 0.0)
    both = jnp.concatenate([orbs, code], 1).astype(BF16)
    both = jnp.concatenate([both, jnp.zeros((64, 2 * PLANE), BF16)], 0)

    for b in range(PAIRS // BLOCK):
        rows = slice(b * BLOCK, (b + 1) * BLOCK)
        lv = dot(ohl[rows].astype(BF16), both)
        rv = dot(ohr[rows].astype(BF16), both)
        same = lv[:, PLANE:] == rv[:, PLANE:]
        lmv = jnp.where(same, lv[:, :PLANE], 0.0)
        rmv = jnp.where(same, rv[:, :PLANE], 0.0)
        lm[rows] = lmv
        rm[rows] = rmv
        dens = turn_rows(lmv * rmv, offs[rows, 1:2], offs[rows, 2:3], -1)
        dh[rows], dl[rows] = split(dens)

    const1.wait()
    const2.wait()
    for n in range(4):
        cols = slice(n * 256, (n + 1) * 256)
        wh, wl = plane[0, :, cols], plane[1, :, cols]
        modes[:, cols] = dot(dh[...], wh) + dot(dl[...], wh) + dot(dh[...], wl)

    def part_of(ref, r):
        return ref.at[pl.ds(pl.multiple_of(lax.div(r, 8) * PART, 8), PART), pl.ds(pl.multiple_of(lax.rem(r, 8) * 128, 128), 128)]

    def device_of(r):
        return device(lax.div(r, 8), lax.rem(lax.div(r, 2), 4), z, lax.rem(r, 2))

    pltpu.make_async_copy(part_of(modes, rho), lines_in.at[rho], recv3).start()

    @pl.loop(1, 32)
    def _(t):
        r = lax.rem(rho + t, 32)
        pltpu.make_async_remote_copy(part_of(modes, r), lines_in.at[rho], send3, recv3, device_of(r), MESH).start()

    pltpu.make_async_copy(lines_in, lines_in, recv3).wait()

    u, v = lax.div(rho, 8), lax.rem(rho, 8)
    scale = table_ref[:, pl.ds(pl.multiple_of(v * 128, 128), 128)]
    scale = jnp.broadcast_to(scale[:, None, :], (SIDE, 8, 128)).reshape(256, 128)
    for j in range(PART // 8):
        rows = slice(8 * j, 8 * j + 8)
        o1 = offs[pl.ds(pl.multiple_of(u * PART, 8) + 8 * j, 8), 0:1]
        s = turn_lead(lines_in[:, rows, :], o1, -1).reshape(256, 128)
        for way in range(2):
            sh, sl = split(s)
            s = dot(lines[0, way], sh) + dot(lines[0, way], sl) + dot(lines[1, way], sh)
            if way == 0:
                s = s * scale
        lines_out[:, rows, :] = turn_lead(s.reshape(SIDE, 8, 128), o1, 1)

    pltpu.make_async_copy(lines_out.at[rho], part_of(back, rho), recv4).start()

    @pl.loop(1, 32)
    def _(t):
        r = lax.rem(rho + t, 32)
        pltpu.make_async_remote_copy(lines_out.at[r], part_of(back, rho), send4, recv4, device_of(r), MESH).start()

    pltpu.make_async_copy(lines_in.at[pl.ds(0, 31)], lines_in.at[pl.ds(0, 31)], send3).wait()
    pltpu.make_async_copy(back, back, recv4).wait()

    bh, bl = split(back[...])
    dh[...] = bh
    dl[...] = bl
    for n in range(4):
        cols = slice(n * 256, (n + 1) * 256)
        wh, wl = plane[0, cols, :], plane[1, cols, :]
        modes[:, cols] = dot(dh[...], wh, NT) + dot(dl[...], wh, NT) + dot(dh[...], wl, NT)

    total = None
    for b in range(PAIRS // BLOCK):
        rows = slice(b * BLOCK, (b + 1) * BLOCK)
        pot = turn_rows(modes[rows], offs[rows, 1:2], offs[rows, 2:3], 1)
        term = None
        for one, other in ((ohl, rm), (ohr, lm)):
            ch, cl = split(pot * other[rows])
            pick = one[rows].astype(BF16)
            new = dot(pick, ch, TN) + dot(pick, cl, TN)
            term = new if term is None else term + new
        total = term if total is None else total + term
    field[...] = total[0:ORB]
    far_field[...] = total[ORB : 2 * ORB]

    far_copy = pltpu.make_async_remote_copy(far_field, prev_field, send5, recv5, device(x, y, nxt, core), MESH)
    far_copy.start()
    framed = jnp.where(code[:ORB] == code[0:1], orbs[:ORB], 0.0)
    perm_row = iota((128, ORB), 0)
    perm = (lax.rem(perm_row, 8) * 4 + lax.div(perm_row, 8) == iota((128, ORB), 1)) & (perm_row < ORB)
    framed = dot(perm.astype(BF16), framed.astype(BF16)).astype(BF16)
    far_copy.wait_recv()
    summed = field[...] + prev_field[...]
    framed_field = jnp.where(code[:ORB] == code[0:1], summed, 0.0).astype(BF16)
    gp[0:ORB] = dot(framed_field, framed, NT)
    gp[ORB : ORB + 8] = jnp.zeros((8, 128), F32)
    for r in range(8):
        tiles[pl.ds(r, ORB, stride=8), :] = summed[:, r * 128 : (r + 1) * 128]

    home_x, home_zh, home_c = lax.div(role, 4), lax.rem(lax.div(role, 2), 2), lax.rem(role, 2)
    sends6 = []
    for k in range(8):
        send6[k, 0:4] = tiles[32 * k : 32 * k + 32].reshape(4, 8, 128)
        send6[k, 4] = gp[4 * k : 4 * k + 8]
        target = home_zh * 8 + k
        here = jnp.logical_and(target == z, home_c == core)
        into = mid6.at[home_x * 2 + core]
        remote = pltpu.make_async_remote_copy(
            send6.at[k], into, send6s.at[k], recv6, device(x, y, target, home_c), MESH
        )
        local_copy = pltpu.make_async_copy(send6.at[k], into, recv6)
        pl.when(here)(local_copy.start)
        pl.when(jnp.logical_not(here))(remote.start)
        sends6.append((here, remote))
    pltpu.make_async_copy(mid6, mid6, recv6).wait()
    for g in range(4):
        gram_tile = mid6[2 * g, 4] + mid6[2 * g + 1, 4]
        for j in range(4):
            send7[4 * g + j, 0] = mid6[2 * g, j]
            send7[4 * g + j, 1] = mid6[2 * g + 1, j]
            send7[4 * g + j, 2] = gram_tile
    pltpu.make_async_copy(send7.at[q], fin.at[q], recv7).start()
    for t in range(1, 16):
        peer = lax.rem(q + t, 16)
        pltpu.make_async_remote_copy(
            send7.at[peer], fin.at[q], send7s, recv7, device(lax.div(peer, 4), lax.rem(peer, 4), z, core), MESH
        ).start()
    pltpu.make_async_copy(fin, fin, recv7).wait()
    result = turn_box(fin[:, 0:2].reshape(SIDE, 8, 128), own_o, -1)
    field_ref[...] = result.reshape(256, 128)
    gram_tile = fin[0, 2]
    for k in range(1, 16):
        gram_tile = gram_tile + fin[k, 2]
    gram_tile = jnp.where(iota((8, 128), 0) == y, gram_tile, 0.0)
    gram_ref[...] = jnp.sum(gram_tile, axis=0, keepdims=True) * (1.0 / math.sqrt(CELLS))

    for here, remote in sends2 + sends6:
        pl.when(jnp.logical_not(here))(remote.wait_send)
    pltpu.make_async_copy(lines_in.at[pl.ds(0, 31)], lines_in.at[pl.ds(0, 31)], send4).wait()
    far_copy.wait_send()
    pltpu.make_async_copy(fin.at[pl.ds(0, 15)], fin.at[pl.ds(0, 15)], send7s).wait()


def on_device(orbitals, offsets, slot_pairs):
    plane_c, lines_c, table_c = constants()
    slots = jnp.pad(slot_pairs, ((0, 2), (0, 126)), constant_values=-1)
    vmem = pl.BlockSpec(memory_space=pltpu.VMEM)
    hbm = pl.BlockSpec(memory_space=pl.ANY)
    dma = pltpu.SemaphoreType.DMA
    scratch = [
        pltpu.VMEM((2, PLANE, PLANE), BF16),
        pltpu.VMEM((2, 2, 256, 256), BF16),
        pltpu.VMEM((16, 2, 16, 128), BF16),
        pltpu.VMEM((16, 2, 16, 128), BF16),
        pltpu.VMEM((4, 2, 3, 16, 128), BF16),
        pltpu.VMEM((4, 2, 2, 16, 128), BF16),
        pltpu.VMEM((8, 3, 16, 128), BF16),
        pltpu.VMEM((8, 2, 16, 128), BF16),
        pltpu.VMEM((512, 128), F32),
        pltpu.VMEM((PAIRS, 128), F32),
        pltpu.VMEM((PAIRS, 128), F32),
        pltpu.VMEM((PAIRS, 3), I32),
        pltpu.VMEM((PAIRS, PLANE), F32),
        pltpu.VMEM((PAIRS, PLANE), F32),
        pltpu.VMEM((PAIRS, PLANE), BF16),
        pltpu.VMEM((PAIRS, PLANE), BF16),
        pltpu.VMEM((PAIRS, PLANE), F32),
        pltpu.VMEM((32, PART, 128), F32),
        pltpu.VMEM((32, PART, 128), F32),
        pltpu.VMEM((PAIRS, PLANE), F32),
        pltpu.VMEM((ORB, PLANE), F32),
        pltpu.VMEM((ORB, PLANE), F32),
        pltpu.VMEM((ORB, PLANE), F32),
        pltpu.VMEM((256, 128), F32),
        pltpu.VMEM((ORB + 8, 128), F32),
        pltpu.VMEM((8, 5, 8, 128), F32),
        pltpu.VMEM((8, 5, 8, 128), F32),
        pltpu.VMEM((16, 3, 8, 128), F32),
        pltpu.VMEM((16, 3, 8, 128), F32),
        dma((2,)),
        dma, dma,
        dma((4, 2, 2)), dma((2,)),
        dma, dma,
        dma, dma,
        dma, dma,
        dma((8,)), dma,
        dma, dma,
    ]
    field, gram = pl.pallas_call(
        kernel,
        out_shape=(jax.ShapeDtypeStruct((256, 128), F32), jax.ShapeDtypeStruct((1, 128), F32)),
        in_specs=[vmem, vmem, vmem, hbm, hbm, vmem],
        out_specs=(vmem, vmem),
        scratch_shapes=scratch,
        compiler_params=pltpu.CompilerParams(has_side_effects=True, vmem_limit_bytes=48 * 2**20),
    )(
        orbitals.reshape(256, 128),
        offsets,
        slots,
        jnp.asarray(plane_c),
        jnp.asarray(lines_c),
        jnp.asarray(table_c),
    )
    return field.reshape(1, CELLS), gram[0, :ORB].reshape(1, ORB, 1)


def solution(mesh):
    return jax.shard_map(
        on_device,
        mesh=mesh,
        in_specs=(P(("grp", "slab"), None), P(), P(("grp", "slab"), None)),
        out_specs=(P(("grp", "slab"), None), P("grp", None, "slab")),
        check_vma=False,
    )
```

time: 875 us -> 109 us (0.12)
  the two profiles are of different devices: /device:TPU:6 before, /device:TPU:1 now
where the time goes in v1:
time: 109 us; the launch traced here: 108 us
  Pallas kernels  99.4 us (91%)
  local copies, waits for them, and re-layouts  6.91 us (6%)
  other arithmetic  1.26 us (1%)
    pallas_call x1, Pallas kernels, on_device(): pl.pallas_call(kernel, out_shape=(jax.ShapeDtypeStruct((256, 128), F32),...  99.4 us
    unnamed x9, local copies, waits for them, and re-layouts  6.39 us

profile of v1, /device:TPU:1, one launch (start us, length us, event | category | flops | bytes accessed | tf_op | source)
XLA Modules:
  0.0 108.2 jit_solution(9969100557449903575)
XLA Ops:
  0.6 0.8 copy.8
  1.4 1.3 %reduce = bf16[32768]{0:T(1024)(128)(2,1)S(1)} reduce(bf16[1,32768]{1,0:T(2,128)(2,1)} %param.6, bf16[]{:T(256)} %constant.15), dimensions={0}, to_apply=%param.6.reduce_sub_computation | reduce | bytes 131074 | tf_op args[0]
  2.7 0.8 copy.9.offsets_ref
  3.5 0.0 copy-start
  3.5 2.2 %copy-done = bf16[2,1024,1024]{2,1,0:T(8,128)(2,1)S(1)} copy-done((bf16[2,1024,1024]{2,1,0:T(8,128)(2,1)S(1)}, bf16[2,1024,1024]{2,1,0:T(8,128)(2,1)}, u32[]{:S(2)}) %copy-start) | copy-done | bytes 4194328
  5.7 0.0 copy-start.1
  5.7 1.0 copy-done.1
  6.8 0.0 copy-start.2
  6.8 0.9 copy-done.2
  7.7 99.4 %shard_map.77 = (f32[256,128]{1,0:T(8,128)S(1)}, f32[1,128]{1,0:T(1,128)S(1)}) custom-call(bf16[256,128]{1,0:T(8,128)(2,1)S(1)} %bitcast.4, s32[512,3]{1,0:T(8,128)S(1)} %copy.9.offsets_ref, s32[8,128]{1,0:T(8,128)S(1)} %pad.4.slots_ref, bf16[2,1024,1024]{2,1,0:T(8,128)(2,1)S(1)} %copy-done, bf16[2,2,256,256]{3,2,1,0:T(8,128)(2,1)S(1)} %copy-done.1, ...), custom_call_target="tpu_custom_call" | custom-call | tf_op jit(solution)/shard_map/pallas_call | solution.py:454
  107.1 0.5 slice_bitcast_fusion
  107.6 0.7 copy.11
  (1 shorter events, 0.0 us)
Async XLA Ops:
  3.5 2.2 %copy-start = (bf16[2,1024,1024]{2,1,0:T(8,128)(2,1)S(1)}, bf16[2,1024,1024]{2,1,0:T(8,128)(2,1)}, u32[]{:S(2)}) copy-start(bf16[2,1024,1024]{2,1,0:T(8,128)(2,1)} %constant.8.clone.plane_ref) | copy-start | bytes 12582916
  5.7 1.0 copy-start.1
  6.8 0.9 copy-start.2

commit v2 on v1

v2 whole, which is shorter than its diff:
```python
import math

import jax
import jax.numpy as jnp
import numpy as np
from jax import lax
from jax.experimental import pallas as pl
from jax.experimental.pallas import tpu as pltpu
from jax.sharding import PartitionSpec as P

SIDE = 32
PLANE = SIDE * SIDE
CELLS = SIDE * PLANE
CHEB = 6
GROUPS = 16
ORB = 32
PAIRS = 160
PART = 40
BLOCK = 32
F32, BF16, I32 = jnp.float32, jnp.bfloat16, jnp.int32
MESH = pl.DeviceIdType.MESH

NN = (((1,), (0,)), ((), ()))
NT = (((1,), (1,)), ((), ()))
TN = (((0,), (0,)), ((), ()))


def operator_1d():
    weights = {0: -49.0 / 18.0, 1: 1.5, 2: -0.15, 3: 1.0 / 90.0}
    a = np.zeros((SIDE, SIDE))
    for i in range(SIDE):
        for j in range(SIDE):
            a[i, j] = -weights.get(abs(i - j), 0.0)
    return a


def eigen(a):
    a, n = a.copy(), a.shape[0]
    v = np.eye(n)
    for _ in range(10):
        for p in range(n - 1):
            for q in range(p + 1, n):
                if abs(a[p, q]) < 1e-18:
                    continue
                theta = (a[q, q] - a[p, p]) / (2.0 * a[p, q])
                t = (1.0 if theta >= 0 else -1.0) / (abs(theta) + math.sqrt(theta * theta + 1.0))
                c = 1.0 / math.sqrt(t * t + 1.0)
                s = t * c
                ap, aq = a[:, p].copy(), a[:, q].copy()
                a[:, p], a[:, q] = c * ap - s * aq, s * ap + c * aq
                ap, aq = a[p].copy(), a[q].copy()
                a[p], a[q] = c * ap - s * aq, s * ap + c * aq
                vp, vq = v[:, p].copy(), v[:, q].copy()
                v[:, p], v[:, q] = c * vp - s * vq, s * vp + c * vq
    return np.diag(a).copy(), v


def polynomial(lam):
    low, high = 3.0 * (math.pi / (SIDE + 1)) ** 2, 18.2
    mid, half = 0.5 * (high + low), 0.5 * (high - low)
    alpha, beta = 1.0 / mid, 0.0
    x, res, p = np.zeros_like(lam), np.ones_like(lam), np.zeros_like(lam)
    for k in range(1, CHEB + 1):
        if k > 1:
            beta = 0.5 * (half * alpha) ** 2 if k == 2 else (0.5 * half * alpha) ** 2
            alpha = 1.0 / (mid - beta / alpha)
        p = res + beta * p
        x = x + alpha * p
        res = res - alpha * lam * p
    return x


def halves(a):
    high = a.astype(BF16)
    low = (a - high.astype(np.float64)).astype(BF16)
    return np.stack([high, low])


def constants():
    lam, q = eigen(operator_1d())
    plane = halves(np.kron(q, q))
    lines = halves(np.stack([np.kron(q.T, np.eye(8)), np.kron(q, np.eye(8))]))
    total = lam[:, None, None] + lam[None, :, None] + lam[None, None, :]
    table = polynomial(total).reshape(SIDE, PLANE).astype(np.float32)
    return plane, lines, table


def iota(shape, dim):
    return lax.broadcasted_iota(I32, shape, dim)


def roll(x, n, axis):
    n %= x.shape[axis]
    return pltpu.roll(x, n, axis) if n else x


def lead(x, n):
    n %= x.shape[0]
    return jnp.concatenate([x[x.shape[0] - n :], x[: x.shape[0] - n]], 0) if n else x


def bit(o, b):
    return jnp.bitwise_and(jnp.right_shift(o, b), 1) > 0


def turn_rows(x, o2, o3, sign):
    third = jnp.bitwise_and(iota(x.shape, 1), SIDE - 1)
    b2 = jnp.broadcast_to(o2, x.shape)
    b3 = jnp.broadcast_to(o3, x.shape)
    for b in range(4):
        n = 1 << b
        x = jnp.where(bit(b2, b), roll(x, sign * SIDE * n, 1), x)
        inside = third >= n if sign > 0 else third < SIDE - n
        y = jnp.where(inside, roll(x, sign * n, 1), roll(x, sign * (n - SIDE), 1))
        x = jnp.where(bit(b3, b), y, x)
    return x


def turn_box(x, o, sign):
    o1, o2, o3 = (jnp.broadcast_to(v, x.shape) for v in o)
    lane = iota(x.shape, 2)
    third = jnp.bitwise_and(lane, SIDE - 1)
    for b in range(4):
        n = 1 << b
        x = jnp.where(bit(o1, b), lead(x, sign * n), x)
        if b < 2:
            y = roll(x, sign * SIDE * n, 2)
            kept = lane >= SIDE * n if sign > 0 else lane < 128 - SIDE * n
            y = jnp.where(kept, y, roll(y, sign, 1))
        else:
            y = roll(x, sign * n // 4, 1)
        x = jnp.where(bit(o2, b), y, x)
        inside = third >= n if sign > 0 else third < SIDE - n
        y = jnp.where(inside, roll(x, sign * n, 2), roll(x, sign * (n - SIDE), 2))
        x = jnp.where(bit(o3, b), y, x)
    return x


def turn_lead(x, o1, sign):
    o = jnp.broadcast_to(o1, x.shape[1:])[None]
    for b in range(4):
        x = jnp.where(bit(o, b), lead(x, sign << b if sign > 0 else -(1 << b)), x)
    return x


def split(x):
    high = x.astype(BF16)
    return high, (x - high.astype(F32)).astype(BF16)


def dot(a, b, dims=NN):
    return lax.dot_general(a, b, dims, preferred_element_type=F32)


def rotated(x, y, core, t):
    m = lax.rem(t * 5, 16)
    return (
        lax.rem(x + lax.div(m, 4), 4),
        lax.rem(y + lax.rem(m, 4), 4),
        lax.rem(core + lax.div(t, 16), 2),
    )


def device(x, y, z, c):
    return x * 4 + lax.div(z, 8) * 2 + c, y * 8 + lax.rem(z, 8)


def kernel(
    box_ref, offsets_ref, slots_ref, plane_ref, lines_ref, table_ref,
    field_ref, gram_ref,
    plane, lines, table, own, mid, pair_out, boxes_out, pair_in, near_in, far_in, cells,
    ohl, ohr, offs, lm, rm, dh, dl, eh, el, modes, lines_in, lines_out, back,
    far_field, prev_field, tiles, gp, send6, mid6, fin, gram_out, gram_mid, gram_fwd, gram_fin,
    const_sem, send1, recv1, send2, recv2, send3, recv3, send4, recv4, send5, recv5,
    send6s, recv6, send6g, recv6g, send7s, recv7, send7g, recv7g,
):
    gi, si = lax.axis_index("grp"), lax.axis_index("slab")
    x, zh, core = lax.div(gi, 4), lax.rem(lax.div(gi, 2), 2), lax.rem(gi, 2)
    y, zl = lax.div(si, 8), lax.rem(si, 8)
    z = zh * 8 + zl
    q = x * 4 + y
    rho = q * 2 + core
    role = z
    nxt = lax.rem(role + 1, GROUPS)

    entry = pltpu.get_barrier_semaphore()

    @pl.loop(1, 32)
    def _(t):
        peer = rotated(x, y, core, t)
        pl.semaphore_signal(entry, 1, device_id=device(peer[0], peer[1], z, peer[2]), device_id_type=MESH)

    @pl.loop(1, 16)
    def _(t):
        for c in range(2):
            pl.semaphore_signal(entry, 1, device_id=device(x, y, lax.rem(z + t, 16), c), device_id_type=MESH)

    consts = [
        pltpu.make_async_copy(plane_ref, plane, const_sem.at[0]),
        pltpu.make_async_copy(lines_ref, lines, const_sem.at[1]),
        pltpu.make_async_copy(table_ref, table, const_sem.at[2]),
    ]
    for c in consts:
        c.start()

    row = iota((72, 512), 0)
    local = lax.rem(row, ORB)
    ident = jnp.where(row < ORB, role, nxt) * ORB + lax.rem(local, 4) * 8 + lax.div(local, 4)
    ident = jnp.where(row < 2 * ORB, ident, gi * ORB + si)
    pick = (ident == iota((72, 512), 1)).astype(BF16)
    found = dot(pick, offsets_ref[...].astype(BF16), NT)
    own_o = [found[64:65, d : d + 1].astype(I32).reshape(1, 1, 1) for d in range(3)]

    box = turn_box(box_ref[...].astype(F32).reshape(256, 128).reshape(SIDE, 8, 128), own_o, 1)
    own[:, 0] = box.reshape(16, 16, 128).astype(BF16)
    ids = slots_ref[...]
    side = iota((8, 128), 1)
    slots = jnp.full((8, 128), -1, I32)
    for k in range(6):
        at = iota((8, 128), 0) == k
        for c in range(2):
            one = jnp.broadcast_to(ids[c : c + 1, k : k + 1], (8, 128))
            slots = jnp.where(jnp.logical_and(at, side == c), one, slots)
    member = lax.rem(slots, ORB)
    spot = lax.rem(member, 8) * 4 + lax.div(member, 8)
    spot = spot + jnp.where(lax.div(slots, ORB) == gi, 0, ORB)
    spot = jnp.where(slots >= 0, spot, -1).astype(F32)
    own[:, 1] = jnp.broadcast_to(jnp.concatenate([spot, spot], 0).astype(BF16)[None], (16, 16, 128))

    pltpu.make_async_copy(own.at[q], mid.at[q], recv1).start()
    pl.semaphore_wait(entry, 61)

    @pl.loop(1, 16)
    def _(t):
        px, py, _ = rotated(x, y, core, t)
        pltpu.make_async_remote_copy(
            own.at[px * 4 + py], mid.at[q], send1, recv1, device(px, py, z, core), MESH
        ).start()

    pltpu.make_async_copy(mid, mid, recv1).wait()

    heap = mid[:, 0].astype(F32).reshape(4, 4, 2, 8, 128)
    lists = mid[:, 1].astype(F32)[:, :8].reshape(4, 4, 8, 128)
    row8, lane8 = iota((8, 128), 0), iota((8, 128), 1)
    for g in range(4):
        merged = jnp.where(lane8 < 2, lists[g, 0], 0.0)
        for j in range(1, 4):
            merged = merged + jnp.where(lax.div(lane8, 2) == j, roll(lists[g, j], 2 * j, 1), 0.0)
        spread = merged
        for t in range(1, 6):
            spread = spread + roll(merged, 8 * t, 1)
        spread = jnp.where(lax.div(lane8, 8) == row8, spread, 0.0)
        pair_out[g] = jnp.sum(spread, axis=0, keepdims=True)
        for c in range(2):
            part = heap[g, :, c].reshape(2, 16, 128).astype(BF16)
            boxes_out[g, c] = part
    sends2 = []
    for kind in range(3):
        for k in range(4):
            g = lax.rem(k + zl, 4)
            for c in range(2):
                target = lax.rem(g * 4 + zh * 2 + core + GROUPS - (1 if kind == 2 else 0), GROUPS)
                here = jnp.logical_and(target == z, core == c)
                out = pair_out.at[g] if kind == 0 else boxes_out.at[g, c]
                into = (pair_in, near_in, far_in)[kind].at[zl]
                remote = pltpu.make_async_remote_copy(
                    out, into, send2.at[kind, k, c], recv2.at[kind], device(x, y, target, c), MESH
                )
                local_copy = pltpu.make_async_copy(out, into, recv2.at[kind])
                pl.when(here)(local_copy.start)
                pl.when(jnp.logical_not(here))(remote.start)
                sends2.append((here, remote))
    pltpu.make_async_copy(own.at[pl.ds(0, 15)], own.at[pl.ds(0, 15)], send1).wait()
    pltpu.make_async_copy(pair_in, pair_in, recv2.at[0]).wait()

    lists = pair_in[...].reshape(8, 128)
    spots = [(8 * t + 2 * j) for t in range(6) for j in range(4)]
    left = jnp.concatenate([lists[:, a : a + 1] for a in spots], 0)
    right = jnp.concatenate([lists[:, a + 1 : a + 2] for a in spots], 0)
    live = left >= 0
    live_f = jnp.where(live, 1.0, 0.0)
    before = (iota((192, 192), 1) < iota((192, 192), 0)).astype(BF16)
    rank = dot(before, jnp.broadcast_to(live_f, (192, 128)).astype(BF16))[:, 0:1]
    rank = jnp.where(live, rank, -1.0)
    chosen = (jnp.broadcast_to(rank, (192, 256)) == iota((192, 256), 1).astype(F32)).astype(BF16)
    orbital = iota((192, 128), 1).astype(F32)
    pick_l = (jnp.broadcast_to(left, (192, 128)) == orbital).astype(BF16)
    pick_r = (jnp.broadcast_to(right, (192, 128)) == orbital).astype(BF16)
    one_l = dot(chosen, pick_l, TN)[:PAIRS]
    one_r = dot(chosen, pick_r, TN)[:PAIRS]
    ohl[...] = one_l
    ohr[...] = one_r
    o3 = jnp.concatenate([found[:64], jnp.zeros((64, found.shape[1]), F32)], 0)
    offs[...] = jnp.broadcast_to(dot(one_l.astype(BF16), o3.astype(BF16))[:, :3], (PAIRS, 3)).astype(I32)

    lane = iota((64, PLANE), 1)
    o = [jnp.broadcast_to(found[:64, d : d + 1], (64, PLANE)) for d in range(3)]
    code = jnp.where(rho.astype(F32) < o[0], 1.0, 0.0)
    code = code + jnp.where(lax.div(lane, SIDE).astype(F32) < o[1], 2.0, 0.0)
    code = code + jnp.where(jnp.bitwise_and(lane, SIDE - 1).astype(F32) < o[2], 4.0, 0.0)
    pltpu.make_async_copy(near_in, near_in, recv2.at[1]).wait()
    pltpu.make_async_copy(far_in, far_in, recv2.at[2]).wait()
    cells[0:256] = near_in[...].astype(F32).reshape(256, 128)
    cells[256:512] = far_in[...].astype(F32).reshape(256, 128)
    orbs = jnp.concatenate([cells[pl.ds(r, 64, stride=8), :] for r in range(8)], 1)
    both = jnp.concatenate([orbs, code], 1).astype(BF16)
    both = jnp.concatenate([both, jnp.zeros((64, 2 * PLANE), BF16)], 0)

    for b in range(PAIRS // BLOCK):
        rows = slice(b * BLOCK, (b + 1) * BLOCK)
        lv = dot(ohl[rows].astype(BF16), both)
        rv = dot(ohr[rows].astype(BF16), both)
        same = lv[:, PLANE:] == rv[:, PLANE:]
        lmv = jnp.where(same, lv[:, :PLANE], 0.0)
        rmv = jnp.where(same, rv[:, :PLANE], 0.0)
        lm[rows] = lmv
        rm[rows] = rmv
        dens = turn_rows(lmv * rmv, offs[rows, 1:2], offs[rows, 2:3], -1)
        dh[rows], dl[rows] = split(dens)

    for c in consts:
        c.wait()

    def part_of(ref, r):
        return ref.at[
            pl.ds(pl.multiple_of(lax.div(r, 8) * PART, 8), PART),
            pl.ds(pl.multiple_of(lax.rem(r, 8) * 128, 128), 128),
        ]

    for dy in (2, 1, 3, 0):
        py = lax.rem(y + dy, 4)
        cols = pl.ds(pl.multiple_of(py * 256, 256), 256)
        wh, wl = plane[0, :, cols], plane[1, :, cols]
        modes[:, cols] = dot(dh[...], wh) + dot(dl[...], wh) + dot(dh[...], wl)
        for dx in (2, 1, 3, 0):
            for dc in (1, 0):
                px, pc = lax.rem(x + dx, 4), lax.rem(core + dc, 2)
                r = px * 8 + py * 2 + pc
                if (dx, dy, dc) == (0, 0, 0):
                    pltpu.make_async_copy(part_of(modes, rho), lines_in.at[rho], recv3).start()
                else:
                    pltpu.make_async_remote_copy(
                        part_of(modes, r), lines_in.at[rho], send3, recv3, device(px, py, z, pc), MESH
                    ).start()

    pltpu.make_async_copy(lines_in, lines_in, recv3).wait()

    u, v = lax.div(rho, 8), lax.rem(rho, 8)
    scale = table[:, pl.ds(pl.multiple_of(v * 128, 128), 128)]
    scale = jnp.broadcast_to(scale[:, None, :], (SIDE, 8, 128)).reshape(256, 128)
    for j in range(PART // 8):
        rows = slice(8 * j, 8 * j + 8)
        o1 = offs[pl.ds(pl.multiple_of(u * PART, 8) + 8 * j, 8), 0:1]
        s = turn_lead(lines_in[:, rows, :], o1, -1).reshape(256, 128)
        for way in range(2):
            sh, sl = split(s)
            s = dot(lines[0, way], sh) + dot(lines[0, way], sl) + dot(lines[1, way], sh)
            if way == 0:
                s = s * scale
        lines_out[:, rows, :] = turn_lead(s.reshape(SIDE, 8, 128), o1, 1)

    pltpu.make_async_copy(lines_out.at[rho], part_of(back, rho), recv4).start()

    @pl.loop(1, 32)
    def _(t):
        px, py, pc = rotated(x, y, core, t)
        r = px * 8 + py * 2 + pc
        pltpu.make_async_remote_copy(
            lines_out.at[r], part_of(back, rho), send4, recv4, device(px, py, z, pc), MESH
        ).start()

    pltpu.make_async_copy(lines_in.at[pl.ds(0, 31)], lines_in.at[pl.ds(0, 31)], send3).wait()
    pltpu.make_async_copy(back, back, recv4).wait()

    bh, bl = split(back[...])
    dh[...] = bh
    dl[...] = bl
    for n in range(4):
        cols = slice(n * 256, (n + 1) * 256)
        wh, wl = plane[0, cols, :], plane[1, cols, :]
        modes[:, cols] = dot(dh[...], wh, NT) + dot(dl[...], wh, NT) + dot(dh[...], wl, NT)

    for b in range(PAIRS // BLOCK):
        rows = slice(b * BLOCK, (b + 1) * BLOCK)
        pot = turn_rows(modes[rows], offs[rows, 1:2], offs[rows, 2:3], 1)
        dh[rows], dl[rows] = split(pot * lm[rows])
        eh[rows], el[rows] = split(pot * rm[rows])
    pick_f = ohr[:, ORB : 2 * ORB].astype(BF16)
    far_field[...] = dot(pick_f, dh[...], TN) + dot(pick_f, dl[...], TN)

    far_copy = pltpu.make_async_remote_copy(far_field, prev_field, send5, recv5, device(x, y, nxt, core), MESH)
    far_copy.start()
    pick_f = ohr[:, 0:ORB].astype(BF16)
    total = dot(pick_f, dh[...], TN) + dot(pick_f, dl[...], TN)
    pick_f = ohl[:, 0:ORB].astype(BF16)
    total = total + dot(pick_f, eh[...], TN) + dot(pick_f, el[...], TN)
    framed = jnp.where(code[:ORB] == code[0:1], orbs[:ORB], 0.0)
    perm_row = iota((128, ORB), 0)
    perm = (lax.rem(perm_row, 8) * 4 + lax.div(perm_row, 8) == iota((128, ORB), 1)) & (perm_row < ORB)
    framed = dot(perm.astype(BF16), framed.astype(BF16)).astype(BF16)
    far_copy.wait_recv()
    summed = total + prev_field[...]
    for r in range(8):
        tiles[pl.ds(r, ORB, stride=8), :] = summed[:, r * 128 : (r + 1) * 128]
    send6[...] = tiles[...].reshape(8, 4, 8, 128)

    home_x, home_zh, home_c = lax.div(role, 4), lax.rem(lax.div(role, 2), 2), lax.rem(role, 2)
    sends6 = []

    def along_z(out_of, into, send, recv):
        for t in range(8):
            k = lax.rem(zl + t, 8)
            target = home_zh * 8 + k
            here = jnp.logical_and(target == z, home_c == core)
            remote = pltpu.make_async_remote_copy(
                out_of.at[k], into, send.at[t], recv, device(x, y, target, home_c), MESH
            )
            local_copy = pltpu.make_async_copy(out_of.at[k], into, recv)
            pl.when(here)(local_copy.start)
            pl.when(jnp.logical_not(here))(remote.start)
            sends6.append((here, remote))

    along_z(send6, mid6.at[home_x, :, core], send6s, recv6.at[home_x])
    framed_field = jnp.where(code[:ORB] == code[0:1], summed, 0.0).astype(BF16)
    gp[...] = dot(framed_field, framed, NT)
    packed = jnp.zeros((8, 128), F32)
    for j in range(4):
        packed = jnp.where(lax.div(lane8, ORB) == j, roll(gp[pl.ds(j, 8, stride=4), :], ORB * j, 1), packed)
    for k in range(8):
        gram_out[k] = packed[k : k + 1]
    along_z(gram_out, gram_mid.at[home_x, core], send6g, recv6g)

    for g in range(4):
        pltpu.make_async_copy(mid6.at[g], mid6.at[g], recv6.at[g]).wait()
        for dj in (2, 1, 3, 0):
            j = lax.rem(y + dj, 4)
            out = mid6.at[g, j]
            remote = pltpu.make_async_remote_copy(out, fin.at[q], send7s, recv7, device(g, j, z, core), MESH)
            if dj:
                remote.start()
            else:
                pl.when(x == g)(pltpu.make_async_copy(out, fin.at[q], recv7).start)
                pl.when(x != g)(remote.start)
    pltpu.make_async_copy(gram_mid, gram_mid, recv6g).wait()
    for g in range(4):
        gram_fwd[g] = gram_mid[g, 0] + gram_mid[g, 1]
    gram_fin[q] = gram_fwd[x]

    @pl.loop(1, 16)
    def _(t):
        px, py, _ = rotated(x, y, core, t)
        pltpu.make_async_remote_copy(
            gram_fwd.at[px], gram_fin.at[q], send7g, recv7g, device(px, py, z, core), MESH
        ).start()

    pltpu.make_async_copy(fin, fin, recv7).wait()
    result = turn_box(fin[...].reshape(SIDE, 8, 128), own_o, -1)
    field_ref[...] = result.reshape(256, 128)
    pltpu.make_async_copy(gram_fin.at[pl.ds(0, 15)], gram_fin.at[pl.ds(0, 15)], recv7g).wait()
    gram_row = gram_fin[0]
    for k in range(1, 16):
        gram_row = gram_row + gram_fin[k]
    gram_row = jnp.broadcast_to(gram_row, (8, 128))
    picked = gram_row
    for j in range(1, 4):
        picked = jnp.where(jnp.broadcast_to(y, (8, 128)) == j, roll(gram_row, -ORB * j, 1), picked)
    gram_ref[...] = picked[0:1] * (1.0 / math.sqrt(CELLS))

    for here, remote in sends2 + sends6:
        pl.when(jnp.logical_not(here))(remote.wait_send)
    pltpu.make_async_copy(lines_in.at[pl.ds(0, 31)], lines_in.at[pl.ds(0, 31)], send4).wait()
    far_copy.wait_send()
    pltpu.make_async_copy(fin.at[pl.ds(0, 15)], fin.at[pl.ds(0, 15)], send7s).wait()
    pltpu.make_async_copy(gram_fin.at[pl.ds(0, 15)], gram_fin.at[pl.ds(0, 15)], send7g).wait()


def on_device(orbitals, offsets, slot_pairs):
    plane_c, lines_c, table_c = constants()
    vmem = pl.BlockSpec(memory_space=pltpu.VMEM)
    hbm = pl.BlockSpec(memory_space=pltpu.HBM)
    dma = pltpu.SemaphoreType.DMA
    scratch = [
        pltpu.VMEM((2, PLANE, PLANE), BF16),
        pltpu.VMEM((2, 2, 256, 256), BF16),
        pltpu.VMEM((SIDE, PLANE), F32),
        pltpu.VMEM((16, 2, 16, 128), BF16),
        pltpu.VMEM((16, 2, 16, 128), BF16),
        pltpu.VMEM((4, 1, 128), F32),
        pltpu.VMEM((4, 2, 2, 16, 128), BF16),
        pltpu.VMEM((8, 1, 128), F32),
        pltpu.VMEM((8, 2, 16, 128), BF16),
        pltpu.VMEM((8, 2, 16, 128), BF16),
        pltpu.VMEM((512, 128), F32),
        pltpu.VMEM((PAIRS, 128), F32),
        pltpu.VMEM((PAIRS, 128), F32),
        pltpu.VMEM((PAIRS, 3), I32),
        pltpu.VMEM((PAIRS, PLANE), F32),
        pltpu.VMEM((PAIRS, PLANE), F32),
        pltpu.VMEM((PAIRS, PLANE), BF16),
        pltpu.VMEM((PAIRS, PLANE), BF16),
        pltpu.VMEM((PAIRS, PLANE), BF16),
        pltpu.VMEM((PAIRS, PLANE), BF16),
        pltpu.VMEM((PAIRS, PLANE), F32),
        pltpu.VMEM((32, PART, 128), F32),
        pltpu.VMEM((32, PART, 128), F32),
        pltpu.VMEM((PAIRS, PLANE), F32),
        pltpu.VMEM((ORB, PLANE), F32),
        pltpu.VMEM((ORB, PLANE), F32),
        pltpu.VMEM((256, 128), F32),
        pltpu.VMEM((ORB, 128), F32),
        pltpu.VMEM((8, 4, 8, 128), F32),
        pltpu.VMEM((4, 4, 2, 8, 128), F32),
        pltpu.VMEM((16, 2, 8, 128), F32),
        pltpu.VMEM((8, 1, 128), F32),
        pltpu.VMEM((4, 2, 1, 128), F32),
        pltpu.VMEM((4, 1, 128), F32),
        pltpu.VMEM((16, 1, 128), F32),
        dma((3,)),
        dma, dma,
        dma((3, 4, 2)), dma((3,)),
        dma, dma,
        dma, dma,
        dma, dma,
        dma((8,)), dma((4,)), dma((8,)), dma,
        dma, dma, dma, dma,
    ]
    field, gram = pl.pallas_call(
        kernel,
        out_shape=(jax.ShapeDtypeStruct((256, 128), F32), jax.ShapeDtypeStruct((1, 128), F32)),
        in_specs=[vmem, vmem, vmem, hbm, hbm, hbm],
        out_specs=(vmem, vmem),
        scratch_shapes=scratch,
        compiler_params=pltpu.CompilerParams(has_side_effects=True, collective_id=1, vmem_limit_bytes=63 * 2**20),
    )(
        orbitals,
        offsets.T,
        slot_pairs.T,
        jnp.asarray(plane_c),
        jnp.asarray(lines_c),
        jnp.asarray(table_c),
    )
    return field.reshape(1, CELLS), gram[0, :ORB].reshape(1, ORB, 1)


def solution(mesh):
    return jax.shard_map(
        on_device,
        mesh=mesh,
        in_specs=(P(("grp", "slab"), None), P(), P(("grp", "slab"), None)),
        out_specs=(P(("grp", "slab"), None), P("grp", None, "slab")),
        check_vma=False,
    )
```

time: 109 us -> 91.3 us (0.84)
  the two profiles are of different devices: /device:TPU:1 before, /device:TPU:6 now
where the time goes in v2:
time: 91.3 us; the launch traced here: 89.9 us
  Pallas kernels  86.6 us (95%)
  local copies, waits for them, and re-layouts  2.74 us (3%)
    pallas_call x1, Pallas kernels, on_device(): pl.pallas_call(kernel, out_shape=(jax.ShapeDtypeStruct((256, 128), F32),...  86.6 us

profile of v2, /device:TPU:6, one launch (start us, length us, event | category | flops | bytes accessed | tf_op | source)
XLA Modules:
  0.0 89.9 jit_solution(9030511490802851307)
XLA Ops:
  0.6 86.6 %shard_map.77 = (f32[256,128]{1,0:T(8,128)}, f32[1,128]{1,0:T(1,128)}) custom-call(bf16[1,32768]{1,0:T(2,128)(2,1)} %box_ref.1, s32[3,512]{1,0:T(4,128)} %bitcast.6, s32[2,6]{1,0:T(2,128)} %bitcast.7, bf16[2,1024,1024]{2,1,0:T(8,128)(2,1)} %constant.6.clone.plane_ref, bf16[2,2,256,256]{3,2,1,0:T(8,128)(2,1)} %constant.7.clone.lines_ref, ...), custom_call_target="tpu_custom_call" | custom-call | tf_op jit(solution)/shard_map/pallas_call | solution.py:527
  87.2 1.2 %slice_bitcast_fusion = f32[1,32,1]{1,2,0:T(1,128)} fusion(f32[1,128]{1,0:T(1,128)} %get-tuple-element.5), kind=kLoop, calls=%fused_computation | loop fusion | bytes 256 | tf_op jit(solution)/shard_map/reshape;squeeze | solution.py:542
  88.4 1.6 %copy.9 = f32[1,32768]{1,0:T(1,128)} copy(f32[1,32768]{1,0:T(1,128)} %bitcast.5) | data formatting | bytes 262144

commit v3 on v2

--- a/solution.py
+++ b/solution.py
@@ -15,7 +15,7 @@
 GROUPS = 16
 ORB = 32
 PAIRS = 160
-PART = 40
+PARTS = ((0, 24), (96, 16))
 BLOCK = 32
 F32, BF16, I32 = jnp.float32, jnp.bfloat16, jnp.int32
 MESH = pl.DeviceIdType.MESH
@@ -169,8 +169,8 @@
     box_ref, offsets_ref, slots_ref, plane_ref, lines_ref, table_ref,
     field_ref, gram_ref,
     plane, lines, table, own, mid, pair_out, boxes_out, pair_in, near_in, far_in, cells,
-    ohl, ohr, offs, lm, rm, dh, dl, eh, el, modes, lines_in, lines_out, back,
-    far_field, prev_field, tiles, gp, send6, mid6, fin, gram_out, gram_mid, gram_fwd, gram_fin,
+    ohl, ohr, offs, lm, rm, dh, dl, eh, el, modes, in_a, in_b, out_a, out_b, back, pots,
+    field, far_field, prev_field, tiles, gp, send6, mid6, fin, gram_out, gram_mid, gram_fwd, gram_fin,
     const_sem, send1, recv1, send2, recv2, send3, recv3, send4, recv4, send5, recv5,
     send6s, recv6, send6g, recv6g, send7s, recv7, send7g, recv7g,
 ):
@@ -321,114 +321,132 @@
     for c in consts:
         c.wait()
 
-    def part_of(ref, r):
+    def part_of(ref, r, part):
+        base, size = PARTS[part]
         return ref.at[
-            pl.ds(pl.multiple_of(lax.div(r, 8) * PART, 8), PART),
+            pl.ds(pl.multiple_of(base + lax.div(r, 8) * size, 8), size),
             pl.ds(pl.multiple_of(lax.rem(r, 8) * 128, 128), 128),
         ]
 
-    for dy in (2, 1, 3, 0):
-        py = lax.rem(y + dy, 4)
-        cols = pl.ds(pl.multiple_of(py * 256, 256), 256)
-        wh, wl = plane[0, :, cols], plane[1, :, cols]
-        modes[:, cols] = dot(dh[...], wh) + dot(dl[...], wh) + dot(dh[...], wl)
-        for dx in (2, 1, 3, 0):
-            for dc in (1, 0):
-                px, pc = lax.rem(x + dx, 4), lax.rem(core + dc, 2)
-                r = px * 8 + py * 2 + pc
-                if (dx, dy, dc) == (0, 0, 0):
-                    pltpu.make_async_copy(part_of(modes, rho), lines_in.at[rho], recv3).start()
-                else:
-                    pltpu.make_async_remote_copy(
-                        part_of(modes, r), lines_in.at[rho], send3, recv3, device(px, py, z, pc), MESH
-                    ).start()
-
-    pltpu.make_async_copy(lines_in, lines_in, recv3).wait()
+    lines_in, lines_out = (in_a, in_b), (out_a, out_b)
+    for part, (base, size) in enumerate(PARTS):
+        rows = slice(base, base + 4 * size)
+        landing = lines_in[part].at[rho]
+        for dy in (2, 1, 3, 0):
+            py = lax.rem(y + dy, 4)
+            cols = pl.ds(pl.multiple_of(py * 256, 256), 256)
+            wh, wl = plane[0, :, cols], plane[1, :, cols]
+            modes[rows, cols] = dot(dh[rows], wh) + dot(dl[rows], wh) + dot(dh[rows], wl)
+            for dx in (2, 1, 3, 0):
+                for dc in (1, 0):
+                    px, pc = lax.rem(x + dx, 4), lax.rem(core + dc, 2)
+                    out = part_of(modes, px * 8 + py * 2 + pc, part)
+                    if (dx, dy, dc) == (0, 0, 0):
+                        pltpu.make_async_copy(out, landing, recv3.at[part]).start()
+                    else:
+                        pltpu.make_async_remote_copy(
+                            out, landing, send3.at[part], recv3.at[part], device(px, py, z, pc), MESH
+                        ).start()
 
     u, v = lax.div(rho, 8), lax.rem(rho, 8)
     scale = table[:, pl.ds(pl.multiple_of(v * 128, 128), 128)]
     scale = jnp.broadcast_to(scale[:, None, :], (SIDE, 8, 128)).reshape(256, 128)
-    for j in range(PART // 8):
-        rows = slice(8 * j, 8 * j + 8)
-        o1 = offs[pl.ds(pl.multiple_of(u * PART, 8) + 8 * j, 8), 0:1]
-        s = turn_lead(lines_in[:, rows, :], o1, -1).reshape(256, 128)
-        for way in range(2):
-            sh, sl = split(s)
-            s = dot(lines[0, way], sh) + dot(lines[0, way], sl) + dot(lines[1, way], sh)
-            if way == 0:
-                s = s * scale
-        lines_out[:, rows, :] = turn_lead(s.reshape(SIDE, 8, 128), o1, 1)
-
-    pltpu.make_async_copy(lines_out.at[rho], part_of(back, rho), recv4).start()
-
-    @pl.loop(1, 32)
-    def _(t):
-        px, py, pc = rotated(x, y, core, t)
-        r = px * 8 + py * 2 + pc
-        pltpu.make_async_remote_copy(
-            lines_out.at[r], part_of(back, rho), send4, recv4, device(px, py, z, pc), MESH
-        ).start()
-
-    pltpu.make_async_copy(lines_in.at[pl.ds(0, 31)], lines_in.at[pl.ds(0, 31)], send3).wait()
-    pltpu.make_async_copy(back, back, recv4).wait()
-
-    bh, bl = split(back[...])
-    dh[...] = bh
-    dl[...] = bl
-    for n in range(4):
-        cols = slice(n * 256, (n + 1) * 256)
-        wh, wl = plane[0, cols, :], plane[1, cols, :]
-        modes[:, cols] = dot(dh[...], wh, NT) + dot(dl[...], wh, NT) + dot(dh[...], wl, NT)
-
-    for b in range(PAIRS // BLOCK):
-        rows = slice(b * BLOCK, (b + 1) * BLOCK)
-        pot = turn_rows(modes[rows], offs[rows, 1:2], offs[rows, 2:3], 1)
-        dh[rows], dl[rows] = split(pot * lm[rows])
-        eh[rows], el[rows] = split(pot * rm[rows])
+    for part, (base, size) in enumerate(PARTS):
+        source, result = lines_in[part], lines_out[part]
+        pltpu.make_async_copy(source, source, recv3.at[part]).wait()
+        for j in range(size // 8):
+            rows = slice(8 * j, 8 * j + 8)
+            o1 = offs[pl.ds(pl.multiple_of(base + u * size + 8 * j, 8), 8), 0:1]
+            s = turn_lead(source[:, rows, :], o1, -1).reshape(256, 128)
+            for way in range(2):
+                sh, sl = split(s)
+                s = dot(lines[0, way], sh) + dot(lines[0, way], sl) + dot(lines[1, way], sh)
+                if way == 0:
+                    s = s * scale
+            result[:, rows, :] = turn_lead(s.reshape(SIDE, 8, 128), o1, 1)
+
+        landing = part_of(back, rho, part)
+        pltpu.make_async_copy(result.at[rho], landing, recv4.at[part]).start()
+
+        @pl.loop(1, 32)
+        def _(t):
+            px, py, pc = rotated(x, y, core, t)
+            r = px * 8 + py * 2 + pc
+            pltpu.make_async_remote_copy(
+                result.at[r], landing, send4.at[part], recv4.at[part], device(px, py, z, pc), MESH
+            ).start()
+
+    for part, (base, size) in enumerate(PARTS):
+        rows = slice(base, base + 4 * size)
+        arrived = back.at[pl.ds(base, 4 * size)]
+        pltpu.make_async_copy(arrived, arrived, recv4.at[part]).wait()
+        dh[rows], dl[rows] = split(back[rows])
+        for n in range(4):
+            cols = slice(n * 256, (n + 1) * 256)
+            wh, wl = plane[0, cols, :], plane[1, cols, :]
+            pots[rows, cols] = dot(dh[rows], wh, NT) + dot(dl[rows], wh, NT) + dot(dh[rows], wl, NT)
+        for b in range(4 * size // BLOCK):
+            rows = slice(base + b * BLOCK, base + (b + 1) * BLOCK)
+            pot = turn_rows(pots[rows], offs[rows, 1:2], offs[rows, 2:3], 1)
+            dh[rows], dl[rows] = split(pot * lm[rows])
+            eh[rows], el[rows] = split(pot * rm[rows])
     pick_f = ohr[:, ORB : 2 * ORB].astype(BF16)
     far_field[...] = dot(pick_f, dh[...], TN) + dot(pick_f, dl[...], TN)
 
-    far_copy = pltpu.make_async_remote_copy(far_field, prev_field, send5, recv5, device(x, y, nxt, core), MESH)
-    far_copy.start()
+    far_copies = []
+    for t in range(4):
+        k = lax.rem(lax.div(lax.rem(zl + 1, 8), 2) + t, 4)
+        rows = pl.ds(pl.multiple_of(8 * k, 8), 8)
+        far_copies.append(
+            pltpu.make_async_remote_copy(
+                far_field.at[rows], prev_field.at[rows], send5.at[t], recv5.at[k], device(x, y, nxt, core), MESH
+            )
+        )
+        far_copies[-1].start()
     pick_f = ohr[:, 0:ORB].astype(BF16)
     total = dot(pick_f, dh[...], TN) + dot(pick_f, dl[...], TN)
     pick_f = ohl[:, 0:ORB].astype(BF16)
-    total = total + dot(pick_f, eh[...], TN) + dot(pick_f, el[...], TN)
+    field[...] = total + dot(pick_f, eh[...], TN) + dot(pick_f, el[...], TN)
     framed = jnp.where(code[:ORB] == code[0:1], orbs[:ORB], 0.0)
     perm_row = iota((128, ORB), 0)
     perm = (lax.rem(perm_row, 8) * 4 + lax.div(perm_row, 8) == iota((128, ORB), 1)) & (perm_row < ORB)
     framed = dot(perm.astype(BF16), framed.astype(BF16)).astype(BF16)
-    far_copy.wait_recv()
-    summed = total + prev_field[...]
-    for r in range(8):
-        tiles[pl.ds(r, ORB, stride=8), :] = summed[:, r * 128 : (r + 1) * 128]
-    send6[...] = tiles[...].reshape(8, 4, 8, 128)
-
     home_x, home_zh, home_c = lax.div(role, 4), lax.rem(lax.div(role, 2), 2), lax.rem(role, 2)
     sends6 = []
 
-    def along_z(out_of, into, send, recv):
-        for t in range(8):
-            k = lax.rem(zl + t, 8)
-            target = home_zh * 8 + k
-            here = jnp.logical_and(target == z, home_c == core)
-            remote = pltpu.make_async_remote_copy(
-                out_of.at[k], into, send.at[t], recv, device(x, y, target, home_c), MESH
+    def along_z(out, k, into, send, recv):
+        target = home_zh * 8 + k
+        here = jnp.logical_and(target == z, home_c == core)
+        remote = pltpu.make_async_remote_copy(out, into, send, recv, device(x, y, target, home_c), MESH)
+        pl.when(here)(pltpu.make_async_copy(out, into, recv).start)
+        pl.when(jnp.logical_not(here))(remote.start)
+        sends6.append((here, remote))
+
+    for t in range(4):
+        k = lax.rem(lax.div(zl, 2) + t, 4)
+        rows = pl.ds(pl.multiple_of(8 * k, 8), 8)
+        arrived = prev_field.at[rows]
+        pltpu.make_async_copy(arrived, arrived, recv5.at[k]).wait()
+        summed = field[rows] + prev_field[rows]
+        field[rows] = summed
+        for r in range(8):
+            tiles[pl.ds(r, 8, stride=8), :] = summed[:, r * 128 : (r + 1) * 128]
+        for half in range(2):
+            send6[2 * k + half] = tiles[32 * half : 32 * half + 32].reshape(4, 8, 128)
+            along_z(
+                send6.at[2 * k + half], 2 * k + half, mid6.at[home_x, :, core],
+                send6s.at[2 * t + half], recv6.at[home_x],
             )
-            local_copy = pltpu.make_async_copy(out_of.at[k], into, recv)
-            pl.when(here)(local_copy.start)
-            pl.when(jnp.logical_not(here))(remote.start)
-            sends6.append((here, remote))
-
-    along_z(send6, mid6.at[home_x, :, core], send6s, recv6.at[home_x])
-    framed_field = jnp.where(code[:ORB] == code[0:1], summed, 0.0).astype(BF16)
+    framed_field = jnp.where(code[:ORB] == code[0:1], field[...], 0.0).astype(BF16)
     gp[...] = dot(framed_field, framed, NT)
     packed = jnp.zeros((8, 128), F32)
     for j in range(4):
         packed = jnp.where(lax.div(lane8, ORB) == j, roll(gp[pl.ds(j, 8, stride=4), :], ORB * j, 1), packed)
     for k in range(8):
         gram_out[k] = packed[k : k + 1]
-    along_z(gram_out, gram_mid.at[home_x, core], send6g, recv6g)
+    for t in range(8):
+        k = lax.rem(zl + t, 8)
+        along_z(gram_out.at[k], k, gram_mid.at[home_x, core], send6g.at[t], recv6g)
 
     for g in range(4):
         pltpu.make_async_copy(mid6.at[g], mid6.at[g], recv6.at[g]).wait()
@@ -468,8 +486,12 @@
 
     for here, remote in sends2 + sends6:
         pl.when(jnp.logical_not(here))(remote.wait_send)
-    pltpu.make_async_copy(lines_in.at[pl.ds(0, 31)], lines_in.at[pl.ds(0, 31)], send4).wait()
-    far_copy.wait_send()
+    for part in range(2):
+        sent = lines_in[part].at[pl.ds(0, 31)]
+        pltpu.make_async_copy(sent, sent, send3.at[part]).wait()
+        pltpu.make_async_copy(sent, sent, send4.at[part]).wait()
+    for far_copy in far_copies:
+        far_copy.wait_send()
     pltpu.make_async_copy(fin.at[pl.ds(0, 15)], fin.at[pl.ds(0, 15)], send7s).wait()
     pltpu.make_async_copy(gram_fin.at[pl.ds(0, 15)], gram_fin.at[pl.ds(0, 15)], send7g).wait()
 
@@ -501,12 +523,16 @@
         pltpu.VMEM((PAIRS, PLANE), BF16),
         pltpu.VMEM((PAIRS, PLANE), BF16),
         pltpu.VMEM((PAIRS, PLANE), F32),
-        pltpu.VMEM((32, PART, 128), F32),
-        pltpu.VMEM((32, PART, 128), F32),
+        pltpu.VMEM((32, PARTS[0][1], 128), F32),
+        pltpu.VMEM((32, PARTS[1][1], 128), F32),
+        pltpu.VMEM((32, PARTS[0][1], 128), F32),
+        pltpu.VMEM((32, PARTS[1][1], 128), F32),
+        pltpu.VMEM((PAIRS, PLANE), F32),
         pltpu.VMEM((PAIRS, PLANE), F32),
         pltpu.VMEM((ORB, PLANE), F32),
         pltpu.VMEM((ORB, PLANE), F32),
-        pltpu.VMEM((256, 128), F32),
+        pltpu.VMEM((ORB, PLANE), F32),
+        pltpu.VMEM((64, 128), F32),
         pltpu.VMEM((ORB, 128), F32),
         pltpu.VMEM((8, 4, 8, 128), F32),
         pltpu.VMEM((4, 4, 2, 8, 128), F32),
@@ -518,9 +544,9 @@
         dma((3,)),
         dma, dma,
         dma((3, 4, 2)), dma((3,)),
-        dma, dma,
-        dma, dma,
-        dma, dma,
+        dma((2,)), dma((2,)),
+        dma((2,)), dma((2,)),
+        dma((4,)), dma((4,)),
         dma((8,)), dma((4,)), dma((8,)), dma,
         dma, dma, dma, dma,
     ]

time: 91.3 us -> 87.5 us (0.958)
  Pallas kernels: 86.6 us -> 82.9 us
    pallas_call x1, Pallas kernels: 86.6 us -> 82.9 us  [on_device(): pl.pallas_call(kernel, out_shape=(jax.ShapeDtypeStruct((256, 128), F32),...]
where the time goes in v3:
time: 87.5 us; the launch traced here: 86.3 us
  Pallas kernels  82.9 us (95%)
  local copies, waits for them, and re-layouts  2.74 us (3%)
    pallas_call x1, Pallas kernels, on_device(): pl.pallas_call(kernel, out_shape=(jax.ShapeDtypeStruct((256, 128), F32),...  82.9 us

profile of v3, /device:TPU:6, one launch (start us, length us, event | category | flops | bytes accessed | tf_op | source)
XLA Modules:
  0.0 86.3 jit_solution(17183444216203184390)
XLA Ops:
  0.6 82.9 %shard_map.77 = (f32[256,128]{1,0:T(8,128)}, f32[1,128]{1,0:T(1,128)}) custom-call(bf16[1,32768]{1,0:T(2,128)(2,1)} %box_ref.1, s32[3,512]{1,0:T(4,128)} %bitcast.6, s32[2,6]{1,0:T(2,128)} %bitcast.7, bf16[2,1024,1024]{2,1,0:T(8,128)(2,1)} %constant.6.clone.plane_ref, bf16[2,2,256,256]{3,2,1,0:T(8,128)(2,1)} %constant.7.clone.lines_ref, ...), custom_call_target="tpu_custom_call" | custom-call | tf_op jit(solution)/shard_map/pallas_call | solution.py:553
  83.5 1.2 %slice_bitcast_fusion = f32[1,32,1]{1,2,0:T(1,128)} fusion(f32[1,128]{1,0:T(1,128)} %get-tuple-element.5), kind=kLoop, calls=%fused_computation | loop fusion | bytes 256 | tf_op jit(solution)/shard_map/reshape;squeeze | solution.py:568
  84.7 1.6 %copy.9 = f32[1,32768]{1,0:T(1,128)} copy(f32[1,32768]{1,0:T(1,128)} %bitcast.5) | data formatting | bytes 262144

commit v4 on v3

--- a/solution.py
+++ b/solution.py
@@ -170,9 +170,9 @@
     field_ref, gram_ref,
     plane, lines, table, own, mid, pair_out, boxes_out, pair_in, near_in, far_in, cells,
     ohl, ohr, offs, lm, rm, dh, dl, eh, el, modes, in_a, in_b, out_a, out_b, back, pots,
-    field, far_field, prev_field, tiles, gp, send6, mid6, fin, gram_out, gram_mid, gram_fwd, gram_fin,
+    field, far_field, prev_field, tiles, gp, send6, fin, gram_out, gram_fin,
     const_sem, send1, recv1, send2, recv2, send3, recv3, send4, recv4, send5, recv5,
-    send6s, recv6, send6g, recv6g, send7s, recv7, send7g, recv7g,
+    send6s, recv6, send6g, recv6g,
 ):
     gi, si = lax.axis_index("grp"), lax.axis_index("slab")
     x, zh, core = lax.div(gi, 4), lax.rem(lax.div(gi, 2), 2), lax.rem(gi, 2)
@@ -195,6 +195,16 @@
         for c in range(2):
             pl.semaphore_signal(entry, 1, device_id=device(x, y, lax.rem(z + t, 16), c), device_id_type=MESH)
 
+    @pl.loop(0, 32)
+    def _(t):
+        px, py, pc = lax.div(t, 8), lax.rem(lax.div(t, 2), 4), lax.rem(t, 2)
+        other = jnp.logical_or(gi != z, jnp.logical_or(px * 4 + py != q, pc != core))
+
+        @pl.when(other)
+        def _():
+            pl.semaphore_signal(entry, 1, device_id=device(px, py, gi, pc), device_id_type=MESH)
+
+    served = jnp.where(gi == z, 31, 32)
     consts = [
         pltpu.make_async_copy(plane_ref, plane, const_sem.at[0]),
         pltpu.make_async_copy(lines_ref, lines, const_sem.at[1]),
@@ -228,7 +238,7 @@
     own[:, 1] = jnp.broadcast_to(jnp.concatenate([spot, spot], 0).astype(BF16)[None], (16, 16, 128))
 
     pltpu.make_async_copy(own.at[q], mid.at[q], recv1).start()
-    pl.semaphore_wait(entry, 61)
+    pl.semaphore_wait(entry, 61 + served)
 
     @pl.loop(1, 16)
     def _(t):
@@ -412,79 +422,52 @@
     perm = (lax.rem(perm_row, 8) * 4 + lax.div(perm_row, 8) == iota((128, ORB), 1)) & (perm_row < ORB)
     framed = dot(perm.astype(BF16), framed.astype(BF16)).astype(BF16)
     home_x, home_zh, home_c = lax.div(role, 4), lax.rem(lax.div(role, 2), 2), lax.rem(role, 2)
-    sends6 = []
-
-    def along_z(out, k, into, send, recv):
-        target = home_zh * 8 + k
-        here = jnp.logical_and(target == z, home_c == core)
-        remote = pltpu.make_async_remote_copy(out, into, send, recv, device(x, y, target, home_c), MESH)
+    home_g = home_x * 4 + home_zh * 2 + home_c
+
+    def send_home(k, j, out, into, send, recv):
+        here = jnp.logical_and(home_g == gi, j * 8 + k == si)
+        remote = pltpu.make_async_remote_copy(out, into, send, recv, (home_g, j * 8 + k), MESH)
         pl.when(here)(pltpu.make_async_copy(out, into, recv).start)
         pl.when(jnp.logical_not(here))(remote.start)
-        sends6.append((here, remote))
 
     for t in range(4):
-        k = lax.rem(lax.div(zl, 2) + t, 4)
-        rows = pl.ds(pl.multiple_of(8 * k, 8), 8)
+        pair = lax.rem(lax.div(zl, 2) + t, 4)
+        rows = pl.ds(pl.multiple_of(8 * pair, 8), 8)
         arrived = prev_field.at[rows]
-        pltpu.make_async_copy(arrived, arrived, recv5.at[k]).wait()
+        pltpu.make_async_copy(arrived, arrived, recv5.at[pair]).wait()
         summed = field[rows] + prev_field[rows]
         field[rows] = summed
         for r in range(8):
             tiles[pl.ds(r, 8, stride=8), :] = summed[:, r * 128 : (r + 1) * 128]
-        for half in range(2):
-            send6[2 * k + half] = tiles[32 * half : 32 * half + 32].reshape(4, 8, 128)
-            along_z(
-                send6.at[2 * k + half], 2 * k + half, mid6.at[home_x, :, core],
-                send6s.at[2 * t + half], recv6.at[home_x],
-            )
+        send6[pl.ds(pl.multiple_of(8 * pair, 8), 8)] = tiles[...].reshape(8, 8, 128)
+
+        @pl.loop(0, 8)
+        def _(i):
+            k, j = 2 * pair + lax.rem(i, 2), lax.rem(y + lax.div(i, 2), 4)
+            send_home(k, j, send6.at[4 * k + j], fin.at[rho], send6s, recv6)
+
     framed_field = jnp.where(code[:ORB] == code[0:1], field[...], 0.0).astype(BF16)
     gp[...] = dot(framed_field, framed, NT)
-    packed = jnp.zeros((8, 128), F32)
-    for j in range(4):
-        packed = jnp.where(lax.div(lane8, ORB) == j, roll(gp[pl.ds(j, 8, stride=4), :], ORB * j, 1), packed)
-    for k in range(8):
-        gram_out[k] = packed[k : k + 1]
-    for t in range(8):
-        k = lax.rem(zl + t, 8)
-        along_z(gram_out.at[k], k, gram_mid.at[home_x, core], send6g.at[t], recv6g)
-
-    for g in range(4):
-        pltpu.make_async_copy(mid6.at[g], mid6.at[g], recv6.at[g]).wait()
-        for dj in (2, 1, 3, 0):
-            j = lax.rem(y + dj, 4)
-            out = mid6.at[g, j]
-            remote = pltpu.make_async_remote_copy(out, fin.at[q], send7s, recv7, device(g, j, z, core), MESH)
-            if dj:
-                remote.start()
-            else:
-                pl.when(x == g)(pltpu.make_async_copy(out, fin.at[q], recv7).start)
-                pl.when(x != g)(remote.start)
-    pltpu.make_async_copy(gram_mid, gram_mid, recv6g).wait()
-    for g in range(4):
-        gram_fwd[g] = gram_mid[g, 0] + gram_mid[g, 1]
-    gram_fin[q] = gram_fwd[x]
-
-    @pl.loop(1, 16)
-    def _(t):
-        px, py, _ = rotated(x, y, core, t)
-        pltpu.make_async_remote_copy(
-            gram_fwd.at[px], gram_fin.at[q], send7g, recv7g, device(px, py, z, core), MESH
-        ).start()
-
-    pltpu.make_async_copy(fin, fin, recv7).wait()
-    result = turn_box(fin[...].reshape(SIDE, 8, 128), own_o, -1)
-    field_ref[...] = result.reshape(256, 128)
-    pltpu.make_async_copy(gram_fin.at[pl.ds(0, 15)], gram_fin.at[pl.ds(0, 15)], recv7g).wait()
-    gram_row = gram_fin[0]
-    for k in range(1, 16):
-        gram_row = gram_row + gram_fin[k]
-    gram_row = jnp.broadcast_to(gram_row, (8, 128))
-    picked = gram_row
-    for j in range(1, 4):
-        picked = jnp.where(jnp.broadcast_to(y, (8, 128)) == j, roll(gram_row, -ORB * j, 1), picked)
-    gram_ref[...] = picked[0:1] * (1.0 / math.sqrt(CELLS))
-
-    for here, remote in sends2 + sends6:
+    for k in range(ORB):
+        gram_out[k] = gp[k : k + 1]
+
+    @pl.loop(0, ORB)
+    def _(i):
+        k, j = lax.rem(zl + lax.rem(i, 8), 8), lax.rem(y + lax.div(i, 8), 4)
+        send_home(k, j, gram_out.at[4 * k + j], gram_fin.at[rho], send6g, recv6g)
+
+    pltpu.make_async_copy(fin, fin, recv6).wait()
+    field_ref[...] = turn_box(fin[...], own_o, -1).reshape(256, 128)
+    pltpu.make_async_copy(gram_fin, gram_fin, recv6g).wait()
+    gram_ref[...] = jnp.sum(gram_fin[...], axis=0) * (1.0 / math.sqrt(CELLS))
+
+    rest = pl.ds(0, 31)
+    for sent, sem in ((fin, send6s), (gram_fin, send6g)):
+        pltpu.make_async_copy(sent.at[rest], sent.at[rest], sem).wait()
+        one = pltpu.make_async_copy(sent.at[0], sent.at[0], sem)
+        pl.when(home_g != gi)(one.wait)
+
+    for here, remote in sends2:
         pl.when(jnp.logical_not(here))(remote.wait_send)
     for part in range(2):
         sent = lines_in[part].at[pl.ds(0, 31)]
@@ -492,8 +475,6 @@
         pltpu.make_async_copy(sent, sent, send4.at[part]).wait()
     for far_copy in far_copies:
         far_copy.wait_send()
-    pltpu.make_async_copy(fin.at[pl.ds(0, 15)], fin.at[pl.ds(0, 15)], send7s).wait()
-    pltpu.make_async_copy(gram_fin.at[pl.ds(0, 15)], gram_fin.at[pl.ds(0, 15)], send7g).wait()
 
 
 def on_device(orbitals, offsets, slot_pairs):
@@ -534,20 +515,16 @@
         pltpu.VMEM((ORB, PLANE), F32),
         pltpu.VMEM((64, 128), F32),
         pltpu.VMEM((ORB, 128), F32),
-        pltpu.VMEM((8, 4, 8, 128), F32),
-        pltpu.VMEM((4, 4, 2, 8, 128), F32),
-        pltpu.VMEM((16, 2, 8, 128), F32),
-        pltpu.VMEM((8, 1, 128), F32),
-        pltpu.VMEM((4, 2, 1, 128), F32),
-        pltpu.VMEM((4, 1, 128), F32),
-        pltpu.VMEM((16, 1, 128), F32),
+        pltpu.VMEM((ORB, 8, 128), F32),
+        pltpu.VMEM((32, 8, 128), F32),
+        pltpu.VMEM((ORB, 1, 128), F32),
+        pltpu.VMEM((32, 1, 128), F32),
         dma((3,)),
         dma, dma,
         dma((3, 4, 2)), dma((3,)),
         dma((2,)), dma((2,)),
         dma((2,)), dma((2,)),
         dma((4,)), dma((4,)),
-        dma((8,)), dma((4,)), dma((8,)), dma,
         dma, dma, dma, dma,
     ]
     field, gram = pl.pallas_call(

time: 87.5 us -> 84.5 us (0.966)
  Pallas kernels: 82.9 us -> 80.2 us
    pallas_call x1, Pallas kernels: 82.9 us -> 80.2 us  [on_device(): pl.pallas_call(kernel, out_shape=(jax.ShapeDtypeStruct((256, 128), F32),...]
where the time goes in v4:
time: 84.5 us; the launch traced here: 83.6 us
  Pallas kernels  80.2 us (95%)
  local copies, waits for them, and re-layouts  2.74 us (3%)
    pallas_call x1, Pallas kernels, on_device(): pl.pallas_call(kernel, out_shape=(jax.ShapeDtypeStruct((256, 128), F32),...  80.2 us

profile of v4, /device:TPU:6, one launch (start us, length us, event | category | flops | bytes accessed | tf_op | source)
XLA Modules:
  0.0 83.6 jit_solution(14398930725546924178)
XLA Ops:
  0.6 80.2 %shard_map.77 = (f32[256,128]{1,0:T(8,128)}, f32[1,128]{1,0:T(1,128)}) custom-call(bf16[1,32768]{1,0:T(2,128)(2,1)} %box_ref.1, s32[3,512]{1,0:T(4,128)} %bitcast.6, s32[2,6]{1,0:T(2,128)} %bitcast.7, bf16[2,1024,1024]{2,1,0:T(8,128)(2,1)} %constant.6.clone.plane_ref, bf16[2,2,256,256]{3,2,1,0:T(8,128)(2,1)} %constant.7.clone.lines_ref, ...), custom_call_target="tpu_custom_call" | custom-call | tf_op jit(solution)/shard_map/pallas_call | solution.py:530
  80.8 1.2 %slice_bitcast_fusion = f32[1,32,1]{1,2,0:T(1,128)} fusion(f32[1,128]{1,0:T(1,128)} %get-tuple-element.5), kind=kLoop, calls=%fused_computation | loop fusion | bytes 256 | tf_op jit(solution)/shard_map/reshape;squeeze | solution.py:545
  82.0 1.6 %copy.9 = f32[1,32768]{1,0:T(1,128)} copy(f32[1,32768]{1,0:T(1,128)} %bitcast.5) | data formatting | bytes 262144

commit v5 on v4

--- a/solution.py
+++ b/solution.py
@@ -15,7 +15,8 @@
 GROUPS = 16
 ORB = 32
 PAIRS = 160
-PARTS = ((0, 24), (96, 16))
+SIZES = (8, 16, 16)
+PARTS = tuple((4 * sum(SIZES[:i]), n) for i, n in enumerate(SIZES))
 BLOCK = 32
 F32, BF16, I32 = jnp.float32, jnp.bfloat16, jnp.int32
 MESH = pl.DeviceIdType.MESH
@@ -79,7 +80,7 @@
 def constants():
     lam, q = eigen(operator_1d())
     plane = halves(np.kron(q, q))
-    lines = halves(np.stack([np.kron(q.T, np.eye(8)), np.kron(q, np.eye(8))]))
+    lines = np.stack([halves(np.kron(q.T, np.eye(8))), halves(np.kron(q, np.eye(8)))])
     total = lam[:, None, None] + lam[None, :, None] + lam[None, None, :]
     table = polynomial(total).reshape(SIDE, PLANE).astype(np.float32)
     return plane, lines, table
@@ -152,6 +153,12 @@
     return lax.dot_general(a, b, dims, preferred_element_type=F32)
 
 
+def three(high, low, matrix_high, matrix_low, dims=NN):
+    n = high.shape[0]
+    both = dot(jnp.concatenate([high, low], 0), matrix_high, dims)
+    return both[:n] + both[n:] + dot(high, matrix_low, dims)
+
+
 def rotated(x, y, core, t):
     m = lax.rem(t * 5, 16)
     return (
@@ -169,7 +176,7 @@
     box_ref, offsets_ref, slots_ref, plane_ref, lines_ref, table_ref,
     field_ref, gram_ref,
     plane, lines, table, own, mid, pair_out, boxes_out, pair_in, near_in, far_in, cells,
-    ohl, ohr, offs, lm, rm, dh, dl, eh, el, modes, in_a, in_b, out_a, out_b, back, pots,
+    ohl, ohr, offs, lm, rm, dh, dl, eh, el, modes, lines_in, lines_out, back, pots,
     field, far_field, prev_field, tiles, gp, send6, fin, gram_out, gram_fin,
     const_sem, send1, recv1, send2, recv2, send3, recv3, send4, recv4, send5, recv5,
     send6s, recv6, send6g, recv6g,
@@ -338,15 +345,18 @@
             pl.ds(pl.multiple_of(lax.rem(r, 8) * 128, 128), 128),
         ]
 
-    lines_in, lines_out = (in_a, in_b), (out_a, out_b)
+    def piece(ref, part, at=slice(None)):
+        base, size = PARTS[part]
+        return ref.at[at, base // 4 : base // 4 + size]
+
     for part, (base, size) in enumerate(PARTS):
         rows = slice(base, base + 4 * size)
-        landing = lines_in[part].at[rho]
+        landing = piece(lines_in, part, rho)
         for dy in (2, 1, 3, 0):
             py = lax.rem(y + dy, 4)
             cols = pl.ds(pl.multiple_of(py * 256, 256), 256)
             wh, wl = plane[0, :, cols], plane[1, :, cols]
-            modes[rows, cols] = dot(dh[rows], wh) + dot(dl[rows], wh) + dot(dh[rows], wl)
+            modes[rows, cols] = three(dh[rows], dl[rows], wh, wl)
             for dx in (2, 1, 3, 0):
                 for dc in (1, 0):
                     px, pc = lax.rem(x + dx, 4), lax.rem(core + dc, 2)
@@ -362,28 +372,28 @@
     scale = table[:, pl.ds(pl.multiple_of(v * 128, 128), 128)]
     scale = jnp.broadcast_to(scale[:, None, :], (SIDE, 8, 128)).reshape(256, 128)
     for part, (base, size) in enumerate(PARTS):
-        source, result = lines_in[part], lines_out[part]
-        pltpu.make_async_copy(source, source, recv3.at[part]).wait()
+        pltpu.make_async_copy(piece(lines_in, part), piece(lines_in, part), recv3.at[part]).wait()
         for j in range(size // 8):
-            rows = slice(8 * j, 8 * j + 8)
+            rows = slice(base // 4 + 8 * j, base // 4 + 8 * j + 8)
             o1 = offs[pl.ds(pl.multiple_of(base + u * size + 8 * j, 8), 8), 0:1]
-            s = turn_lead(source[:, rows, :], o1, -1).reshape(256, 128)
+            s = turn_lead(lines_in[:, rows, :], o1, -1).reshape(256, 128)
             for way in range(2):
                 sh, sl = split(s)
-                s = dot(lines[0, way], sh) + dot(lines[0, way], sl) + dot(lines[1, way], sh)
+                both = dot(lines[way].reshape(512, 256), sh)
+                s = both[:256] + both[256:] + dot(lines[way, 0], sl)
                 if way == 0:
                     s = s * scale
-            result[:, rows, :] = turn_lead(s.reshape(SIDE, 8, 128), o1, 1)
+            lines_out[:, rows, :] = turn_lead(s.reshape(SIDE, 8, 128), o1, 1)
 
         landing = part_of(back, rho, part)
-        pltpu.make_async_copy(result.at[rho], landing, recv4.at[part]).start()
+        pltpu.make_async_copy(piece(lines_out, part, rho), landing, recv4.at[part]).start()
 
         @pl.loop(1, 32)
         def _(t):
             px, py, pc = rotated(x, y, core, t)
             r = px * 8 + py * 2 + pc
             pltpu.make_async_remote_copy(
-                result.at[r], landing, send4.at[part], recv4.at[part], device(px, py, z, pc), MESH
+                piece(lines_out, part, r), landing, send4.at[part], recv4.at[part], device(px, py, z, pc), MESH
             ).start()
 
     for part, (base, size) in enumerate(PARTS):
@@ -394,7 +404,7 @@
         for n in range(4):
             cols = slice(n * 256, (n + 1) * 256)
             wh, wl = plane[0, cols, :], plane[1, cols, :]
-            pots[rows, cols] = dot(dh[rows], wh, NT) + dot(dl[rows], wh, NT) + dot(dh[rows], wl, NT)
+            pots[rows, cols] = three(dh[rows], dl[rows], wh, wl, NT)
         for b in range(4 * size // BLOCK):
             rows = slice(base + b * BLOCK, base + (b + 1) * BLOCK)
             pot = turn_rows(pots[rows], offs[rows, 1:2], offs[rows, 2:3], 1)
@@ -469,8 +479,8 @@
 
     for here, remote in sends2:
         pl.when(jnp.logical_not(here))(remote.wait_send)
-    for part in range(2):
-        sent = lines_in[part].at[pl.ds(0, 31)]
+    for part in range(len(PARTS)):
+        sent = piece(lines_in, part, pl.ds(0, 31))
         pltpu.make_async_copy(sent, sent, send3.at[part]).wait()
         pltpu.make_async_copy(sent, sent, send4.at[part]).wait()
     for far_copy in far_copies:
@@ -504,10 +514,8 @@
         pltpu.VMEM((PAIRS, PLANE), BF16),
         pltpu.VMEM((PAIRS, PLANE), BF16),
         pltpu.VMEM((PAIRS, PLANE), F32),
-        pltpu.VMEM((32, PARTS[0][1], 128), F32),
-        pltpu.VMEM((32, PARTS[1][1], 128), F32),
-        pltpu.VMEM((32, PARTS[0][1], 128), F32),
-        pltpu.VMEM((32, PARTS[1][1], 128), F32),
+        pltpu.VMEM((32, 40, 128), F32),
+        pltpu.VMEM((32, 40, 128), F32),
         pltpu.VMEM((PAIRS, PLANE), F32),
         pltpu.VMEM((PAIRS, PLANE), F32),
         pltpu.VMEM((ORB, PLANE), F32),
@@ -522,8 +530,8 @@
         dma((3,)),
         dma, dma,
         dma((3, 4, 2)), dma((3,)),
-        dma((2,)), dma((2,)),
-        dma((2,)), dma((2,)),
+        dma((len(PARTS),)), dma((len(PARTS),)),
+        dma((len(PARTS),)), dma((len(PARTS),)),
         dma((4,)), dma((4,)),
         dma, dma, dma, dma,
     ]

time: 84.5 us -> 81 us (0.959)
  Pallas kernels: 80.2 us -> 77.5 us
    pallas_call x1, Pallas kernels: 80.2 us -> 77.5 us  [on_device(): pl.pallas_call(kernel, out_shape=(jax.ShapeDtypeStruct((256, 128), F32),...]
where the time goes in v5:
time: 81 us; the launch traced here: 80.8 us
  Pallas kernels  77.5 us (96%)
  local copies, waits for them, and re-layouts  2.74 us (3%)
    pallas_call x1, Pallas kernels, on_device(): pl.pallas_call(kernel, out_shape=(jax.ShapeDtypeStruct((256, 128), F32),...  77.5 us

profile of v5, /device:TPU:6, one launch (start us, length us, event | category | flops | bytes accessed | tf_op | source)
XLA Modules:
  0.0 80.8 jit_solution(13327375233708470227)
XLA Ops:
  0.6 77.5 %shard_map.77 = (f32[256,128]{1,0:T(8,128)}, f32[1,128]{1,0:T(1,128)}) custom-call(bf16[1,32768]{1,0:T(2,128)(2,1)} %box_ref.1, s32[3,512]{1,0:T(4,128)} %bitcast.6, s32[2,6]{1,0:T(2,128)} %bitcast.7, bf16[2,1024,1024]{2,1,0:T(8,128)(2,1)} %constant.6.clone.plane_ref, bf16[2,2,256,256]{3,2,1,0:T(8,128)(2,1)} %constant.7.clone.lines_ref, ...), custom_call_target="tpu_custom_call" | custom-call | tf_op jit(solution)/shard_map/pallas_call | solution.py:538
  78.1 1.2 %slice_bitcast_fusion = f32[1,32,1]{1,2,0:T(1,128)} fusion(f32[1,128]{1,0:T(1,128)} %get-tuple-element.5), kind=kLoop, calls=%fused_computation | loop fusion | bytes 256 | tf_op jit(solution)/shard_map/reshape;squeeze | solution.py:553
  79.3 1.6 %copy.9 = f32[1,32768]{1,0:T(1,128)} copy(f32[1,32768]{1,0:T(1,128)} %bitcast.5) | data formatting | bytes 262144

commit v6 on v5

--- a/solution.py
+++ b/solution.py
@@ -408,11 +408,12 @@
         for b in range(4 * size // BLOCK):
             rows = slice(base + b * BLOCK, base + (b + 1) * BLOCK)
             pot = turn_rows(pots[rows], offs[rows, 1:2], offs[rows, 2:3], 1)
+            pots[rows] = pot
             dh[rows], dl[rows] = split(pot * lm[rows])
-            eh[rows], el[rows] = split(pot * rm[rows])
-    pick_f = ohr[:, ORB : 2 * ORB].astype(BF16)
-    far_field[...] = dot(pick_f, dh[...], TN) + dot(pick_f, dl[...], TN)
-
+        rows = slice(base, base + 4 * size)
+        pick_f = ohr[rows, ORB : 2 * ORB].astype(BF16)
+        term = dot(pick_f, dh[rows], TN) + dot(pick_f, dl[rows], TN)
+        far_field[...] = far_field[...] + term if part else term
     far_copies = []
     for t in range(4):
         k = lax.rem(lax.div(lax.rem(zl + 1, 8), 2) + t, 4)
@@ -425,6 +426,9 @@
         far_copies[-1].start()
     pick_f = ohr[:, 0:ORB].astype(BF16)
     total = dot(pick_f, dh[...], TN) + dot(pick_f, dl[...], TN)
+    for b in range(PAIRS // BLOCK):
+        rows = slice(b * BLOCK, (b + 1) * BLOCK)
+        eh[rows], el[rows] = split(pots[rows] * rm[rows])
     pick_f = ohl[:, 0:ORB].astype(BF16)
     field[...] = total + dot(pick_f, eh[...], TN) + dot(pick_f, el[...], TN)
     framed = jnp.where(code[:ORB] == code[0:1], orbs[:ORB], 0.0)

time: 81 us -> 81 us (level)
  no operation moved by 1% of the time
where the time goes in v6:
time: 81 us; the launch traced here: 80.8 us
  Pallas kernels  77.4 us (96%)
  local copies, waits for them, and re-layouts  2.74 us (3%)
    pallas_call x1, Pallas kernels, on_device(): pl.pallas_call(kernel, out_shape=(jax.ShapeDtypeStruct((256, 128), F32),...  77.4 us

profile of v6, /device:TPU:6, one launch (start us, length us, event | category | flops | bytes accessed | tf_op | source)
XLA Modules:
  0.0 80.8 jit_solution(16484977950533325008)
XLA Ops:
  0.6 77.4 %shard_map.77 = (f32[256,128]{1,0:T(8,128)}, f32[1,128]{1,0:T(1,128)}) custom-call(bf16[1,32768]{1,0:T(2,128)(2,1)} %box_ref.1, s32[3,512]{1,0:T(4,128)} %bitcast.6, s32[2,6]{1,0:T(2,128)} %bitcast.7, bf16[2,1024,1024]{2,1,0:T(8,128)(2,1)} %constant.6.clone.plane_ref, bf16[2,2,256,256]{3,2,1,0:T(8,128)(2,1)} %constant.7.clone.lines_ref, ...), custom_call_target="tpu_custom_call" | custom-call | tf_op jit(solution)/shard_map/pallas_call | solution.py:542
  78.0 1.2 %slice_bitcast_fusion = f32[1,32,1]{1,2,0:T(1,128)} fusion(f32[1,128]{1,0:T(1,128)} %get-tuple-element.5), kind=kLoop, calls=%fused_computation | loop fusion | bytes 256 | tf_op jit(solution)/shard_map/reshape;squeeze | solution.py:557
  79.2 1.6 %copy.9 = f32[1,32768]{1,0:T(1,128)} copy(f32[1,32768]{1,0:T(1,128)} %bitcast.5) | data formatting | bytes 262144
